TPU v7x, 1024 devices: a whole 8x8x8 slice. The times are simulated.
1024 devices in a mesh: dp: 64 (over y, z), feat: 16 (over x, core).
Axes of the slice: x: 8, y: 8, z: 8, core: 2. Of those that a mesh axis runs over, the one named last changes fastest.
Arguments:
- source_feat: bfloat16 [524288, 1024], P('dp', 'feat'), may hold values from -6 to 6
- weight: bfloat16 [1024, 512], P('feat'), may hold values from -0.1875 to 0.1875
- tile_index: int32 [1024, 8], P('dp'), may hold values from 0 to 63
- tile_count: int32 [1024], P('dp'), may hold values from 1 to 8, as said below
- tile_mask: int32 [1024, 8, 128, 128], P('dp'), may hold values 0 or 1
- cotangent: bfloat16 [131072, 512], P(('dp', 'feat')), may hold values from -6 to 6
Outputs:
- hidden: bfloat16 [131072, 512], P(('dp', 'feat'))
- weight_grad: float32 [1024, 512], P('feat')
Inputs may be any that keep to these rules, and one draw needn't show every extreme that they name: `tile_count`: every target block has at least one live slot; in every dp group some blocks have all 8 slots live.
All inputs are finite; a program needn't handle non-finite values. No bound on the sum of `tile_mask` on one device may be relied on, other than what follows from the above.
Results may differ from a plain program's by a relative error of at most 0.0052.
Values may be sent and summed in bfloat16 or wider, within the bound.
A program may use at most 32 MiB of HBM per device.

v0:
```python
import jax
import jax.numpy as jnp
from jax import lax
from jax.sharding import PartitionSpec as P


def activate(z, cotangent):
    sig = jax.nn.sigmoid(z)
    hidden = (z * sig).astype(jnp.bfloat16)
    slope = cotangent.astype(jnp.float32) * sig * (1.0 + z * (1.0 - sig))
    return (hidden, slope.astype(jnp.bfloat16))


def outer_rows(left, right):
    return lax.dot_general(
        left, right, (((0,), (0,)), ((), ())), preferred_element_type=jnp.float32
    )


def shards(source_feat, weight, tile_index, tile_count, tile_mask, cotangent):
    nblk, maxt, tile, _ = tile_mask.shape
    width = source_feat.shape[1]
    blocks = source_feat.reshape(-1, tile, width)
    picked = jnp.take(blocks, tile_index, axis=0)
    slots = lax.broadcasted_iota(jnp.int32, (nblk, maxt), 1)
    live = slots < tile_count[:, None]
    links = jnp.where(live[:, :, None, None], tile_mask, 0)
    degree = jnp.maximum(jnp.sum(links, axis=(1, 3)), 1).astype(jnp.float32)
    summed = jnp.einsum(
        "bsij,bsjf->bif", links.astype(jnp.bfloat16), picked, preferred_element_type=jnp.float32
    )
    agg = (summed / degree[:, :, None]).reshape(nblk * tile, width).astype(jnp.bfloat16)
    z = lax.psum_scatter(
        jnp.dot(agg, weight, preferred_element_type=jnp.float32),
        "feat",
        scatter_dimension=0,
        tiled=True,
    )
    hidden, slope = activate(z, cotangent)
    slope_all = lax.all_gather(slope, "feat", axis=0, tiled=True)
    piece = outer_rows(agg, slope_all)
    weight_grad = lax.psum(piece, "dp")
    return (hidden, weight_grad)


def solution(mesh):
    in_specs = (
        P("dp", "feat"),
        P("feat", None),
        P("dp", None),
        P("dp"),
        P("dp", None, None, None),
        P(("dp", "feat"), None),
    )
    out_specs = (P(("dp", "feat"), None), P("feat", None))
    return jax.shard_map(shards, mesh=mesh, in_specs=in_specs, out_specs=out_specs, check_vma=False)
```

profile of v0, /device:TPU:1, one launch (start us, length us, event | category | flops | bytes accessed | tf_op | source)
XLA Modules:
  0.0 324.0 jit_solution(12778329248252743736)
XLA Ops:
  7.2 0.0 copy-start
  7.2 0.0 reduce-scatter.2.cloned.1.call-start
  7.2 0.8 compare_and_fusion
  8.0 0.7 compare_select_fusion
  8.7 0.1 copy.14
  8.8 0.7 iota_compare_fusion
  9.5 0.1 copy.15
  9.6 0.1 reshape.40
  9.7 4.1 %select_reduce_fusion = s32[16,128]{1,0:T(8,128)S(1)} fusion(s32[16,8,128,128]{3,2,1,0:T(8,128)} %param.10, pred[16,8]{1,0:T(8,128)(4,1)S(1)} %iota_compare_fusion), kind=kLoop, calls=%fused_computation.1 | loop fusion | flops 4192256 | bytes 8396928 | tf_op jit(solution)/shard_map/reduce_sum | solution.py:28
  13.8 0.0 copy-done
  13.8 0.3 copy_bitcast_fusion
  14.1 2.1 gather_fusion
  16.3 0.0 copy-start.2
  16.3 5.7 %fusion.15 = bf16[16,8,8,128]{3,2,1,0:T(8,128)(2,1)S(1)} fusion(bf16[16,8,128,64]{2,3,1,0:T(8,128)(2,1)} %bitcast.24, pred[16,8]{1,0:T(8,128)(4,1)S(1)} %copy.14, s32[16,8,128,128]{3,2,1,0:T(8,128)} %param.10, pred[16,8]{1,0:T(8,128)(4,1)S(1)} %iota_compare_fusion, f32[16,128]{1,0:T(8,128)S(1)} %maximum_convert_fusion), kind=kOutput, calls=%fused_computation.13 | convolution fusion | flops 273940480 | bytes 10756352 | tf_op jit(solution)/shard_map/bsij,bsjf->bif/dot_general | solution.py:29
  21.9 0.0 copy-done.2
  21.9 0.0 copy-start.1
  22.0 2.7 fusion.20
  24.6 0.0 reduce-scatter.2.cloned.1.call-update
  24.7 0.0 all-gather.2.cloned.1.call-start
  24.7 79.5 %reduce-scatter.2.cloned.1.call-done = f32[128,512]{1,0:T(8,128)} async-done(((f32[2048,512]{1,0:T(8,128)}), f32[128,512]{1,0:T(8,128)}) %reduce-scatter.2.cloned.1.call-update) | async-done | bytes 262160 | tf_op jit(solution)/shard_map/reduce_scatter | solution.py:33
  104.2 0.0 copy-done.1
  104.2 1.8 multiply_convert_fusion
  106.0 0.0 all-gather.2.cloned.1.call-update
  106.0 0.0 all-reduce.2.cloned.1.call-start
  106.1 46.3 %all-gather.2.cloned.1.call-done = bf16[2048,512]{1,0:T(8,128)(2,1)} async-done(((bf16[128,512]{1,0:T(8,128)(2,1)}), bf16[2048,512]{1,0:T(8,128)(2,1)}) %all-gather.2.cloned.1.call-update) | async-done | bytes 2097168 | tf_op jit(solution)/shard_map/all_gather | solution.py:40
  152.4 2.7 fusion.18
  155.1 0.0 all-reduce.2.cloned.1.call-update
  155.1 160.7 %all-reduce.2.cloned.1.call-done = f32[64,512]{1,0:T(8,128)} async-done(((f32[64,512]{1,0:T(8,128)}), f32[64,512]{1,0:T(8,128)}) %all-reduce.2.cloned.1.call-update) | async-done | bytes 131088 | tf_op jit(solution)/shard_map/psum | solution.py:42
  315.9 1.6 copy.31
  (2 shorter events, 0.0 us)
Async XLA Ops:
  7.2 6.7 %copy-start = (bf16[8192,64]{0,1:T(8,128)(2,1)S(1)}, bf16[8192,64]{0,1:T(8,128)(2,1)}, u32[]{:S(2)}) copy-start(bf16[8192,64]{0,1:T(8,128)(2,1)} %param.6) | copy-start | bytes 3145732
  7.2 97.0 %reduce-scatter.2.cloned.1.call-start = ((), (), s32[]{:S(2)}) async-start(), calls=%async_computation.1 | async-start | bytes 4456448 | tf_op jit(solution)/shard_map/reduce_scatter | solution.py:33
  16.3 5.7 %copy-start.2 = (bf16[64,512]{1,0:T(8,128)(2,1)S(1)}, bf16[64,512]{1,0:T(8,128)(2,1)}, u32[]{:S(2)}) copy-start(bf16[64,512]{1,0:T(8,128)(2,1)} %param.7) | copy-start | bytes 196612
  21.9 82.3 %copy-start.1 = (bf16[128,512]{1,0:T(8,128)(2,1)S(1)}, bf16[128,512]{1,0:T(8,128)(2,1)}, u32[]{:S(2)}) copy-start(bf16[128,512]{1,0:T(8,128)(2,1)} %param.11) | copy-start | bytes 393220
  24.7 127.7 %all-gather.2.cloned.1.call-start = ((), (), s32[]{:S(2)}) async-start(), calls=%async_computation.2 | async-start | bytes 2228224 | tf_op jit(solution)/shard_map/all_gather | solution.py:40
  106.0 209.9 %all-reduce.2.cloned.1.call-start = ((), (), s32[]{:S(2)}) async-start(), calls=%async_computation.3 | async-start | bytes 262144 | tf_op jit(solution)/shard_map/psum | solution.py:42
Sparse Core Ops, SparseCore 0:
  24.8 79.3 reduce-scatter.1
  107.5 44.8 all-gather.1
  156.2 159.6 all-reduce.1
where the time goes:
time: 328 us; the launch traced here: 324 us
  waiting for transfers between devices  287 us (88%)
  between operations  13.8 us (4%)
  matrix products  11.1 us (3%)
  other arithmetic  8.09 us (2%)
  local copies, waits for them, and re-layouts  4.26 us (1%)
    psum x1, waiting for transfers between devices, shards(): weight_grad = lax.psum(piece, 'dp')  161 us
    reduce_scatter x1, waiting for transfers between devices, shards(): lax.psum_scatter(jnp.dot(agg, weight, preferred_element_type=jnp.float32)...  79.5 us
    all_gather x1, waiting for transfers between devices, shards(): slope_all = lax.all_gather(slope, 'feat', axis=0, tiled=True)  46.3 us
  transfers between devices with their start and end apart: 3, of which 3 were waited for; matrix products, arithmetic and copies ran while one was open for 0% of the time, Pallas kernels for 0%

commit v1 on v0

v1 whole, which is shorter than its diff:
```python
import functools

import jax
import jax.numpy as jnp
from jax import lax
from jax.experimental import pallas as pl
from jax.experimental.pallas import tpu as pltpu
from jax.sharding import PartitionSpec as P

MESH = pl.DeviceIdType.MESH
TILE = 128
AHEAD = 3


def kernel(
    nx, n, maxt, width, tix, tcnt, src, weight, mask, cot, hid_out, wg_out,
    src_v, srcx, mask_v, w_own, cot_own, cot_x, cot_t, w_ab, w_t, agg_send, agg_full,
    hid_buf, hid_rx, p1_send, p1_recv, p2_send, p2_recv, p3_send, p3_recv, res, wg_acc,
    src_sem, mask_sem, w_sem, cot_sem, cx_send, cx_recv, w1_send, w1_recv, w2_send, w2_recv,
    a_send, a_recv, f_send, f_recv, p1_ss, p1_rs, p2_ss, p2_rs, p3_ss, p3_rs, p4_ss, p4_rs, h_send, h_recv,
):
    dp = lax.axis_index("dp")
    feat = lax.axis_index("feat")
    y, z = lax.div(dp, n), lax.rem(dp, n)
    x, c = lax.div(feat, 2), lax.rem(feat, 2)
    half = n // 2
    rows = TILE // n
    place = (y, z)
    f32, bf16 = jnp.float32, jnp.bfloat16

    def at(ab, i):
        return i * n + z if ab == 0 else y * n + i

    def remote(source, target, ssem, rsem, where):
        return pltpu.make_async_remote_copy(
            src_ref=source, dst_ref=target, send_sem=ssem, recv_sem=rsem, device_id=where, device_id_type=MESH
        )

    def each(count, body):
        def step(i, carry):
            body(i)
            return carry

        lax.fori_loop(0, count, step, 0)

    def served(step):
        off = jnp.where(lax.rem(step, 2) == 1, lax.div(nx - 1 - step, 2), nx // 2 + lax.div(step, 2))
        return off

    def mask_copy(step):
        chip = lax.rem(x + served(step), nx)
        return pltpu.make_async_copy(mask.at[pl.ds(2 * chip, 2)], mask_v.at[step], mask_sem.at[step])

    get_src = pltpu.make_async_copy(src, src_v, src_sem)
    get_src.start()
    get_w = pltpu.make_async_copy(weight, w_own, w_sem)
    get_w.start()
    get_cot = pltpu.make_async_copy(cot, cot_own, cot_sem)
    get_cot.start()
    for k in range(min(AHEAD, nx)):
        mask_copy(jnp.int32(k)).start()

    barrier = pltpu.get_barrier_semaphore()

    def greet(where):
        pl.semaphore_signal(barrier, inc=1, device_id=where, device_id_type=MESH)

    def greet_feat(i):
        greet((dp, lax.rem(feat + 1 + i, 2 * nx)))

    def greet_axes(i):
        for ab in (0, 1):
            for core in (0, 1):
                greet((at(ab, lax.rem(place[ab] + 1 + i, n)), 2 * x + core))

    each(2 * nx - 1, greet_feat)
    each(n - 1, greet_axes)

    get_src.wait()
    lane = lax.broadcasted_iota(jnp.int32, (TILE, TILE - width), 1)
    tail = jnp.where(lane == 0, 1.0, 0.0).astype(bf16)

    def widen(i):
        srcx[i] = jnp.concatenate([src_v[i], tail], axis=1)

    each(src_v.shape[0], widen)
    get_w.wait()
    get_cot.wait()

    def w1_copy(ab, to_x, to_c):
        return remote(
            w_own.at[lax.rem(place[ab], half), :, pl.ds(2 * TILE * to_c + TILE * ab, TILE)],
            w_ab.at[ab, x, place[ab]],
            w1_send.at[ab, to_c, to_x],
            w1_recv.at[ab, x],
            (dp, 2 * to_x + to_c),
        )

    def w1_self(ab, from_x):
        return jnp.logical_and(from_x == x, c == lax.div(place[ab], half))

    def send_w1():
        for ab in (0, 1):
            @pl.when(c == lax.div(place[ab], half))
            def _():
                for to_c in (0, 1):
                    def go(to_x):
                        own = jnp.logical_and(to_x == x, to_c == c)

                        @pl.when(jnp.logical_not(own))
                        def _():
                            w1_copy(ab, to_x, to_c).start()

                        @pl.when(own)
                        def _():
                            w_ab[ab, x, place[ab]] = w_own[
                                lax.rem(place[ab], half), :, 2 * TILE * to_c + TILE * ab : 2 * TILE * to_c + TILE * (ab + 1)
                            ]

                    each(nx, go)

    def w1_wait_recv(ab, from_x):
        remote(
            w_own.at[0, :, pl.ds(0, TILE)],
            w_ab.at[ab, from_x, place[ab]],
            w1_send.at[ab, 0, 0],
            w1_recv.at[ab, from_x],
            (dp, feat),
        ).wait_recv()

    def w2_copy(ab, i):
        return remote(
            w_ab.at[ab, :, place[ab]],
            w_ab.at[ab, :, place[ab]],
            w2_send.at[ab, i],
            w2_recv.at[ab, place[ab]],
            (at(ab, i), feat),
        )

    def w2_wait_recv(ab, i):
        remote(
            w_ab.at[ab, :, place[ab]], w_ab.at[ab, :, i], w2_send.at[ab, i], w2_recv.at[ab, i], (at(ab, i), feat)
        ).wait_recv()

    def others(ab, body):
        def go(i):
            body(lax.rem(place[ab] + 1 + i, n))

        each(n - 1, go)

    def send_w2():
        for ab in (0, 1):
            def arrive(from_x):
                @pl.when(jnp.logical_not(w1_self(ab, from_x)))
                def _():
                    w1_wait_recv(ab, from_x)

            each(nx, arrive)
            others(ab, lambda i: w2_copy(ab, i).start())

    def cot_copy():
        return remote(
            cot_own.at[:, pl.ds(pl.multiple_of((1 - c) * 2 * TILE, TILE), 2 * TILE)],
            cot_x.at[c],
            cx_send,
            cx_recv,
            (dp, 2 * x + 1 - c),
        )

    def a_copy(step, to_x):
        return remote(agg_send.at[step], agg_full.at[2 * x + c], a_send.at[step], a_recv.at[x], (dp, 2 * to_x + c))

    def a_wait_recv(from_x):
        remote(
            agg_send.at[0], agg_full.at[2 * from_x + c], a_send.at[0], a_recv.at[from_x], (dp, feat)
        ).wait_recv()

    def f_copy(from_x):
        return remote(
            agg_full.at[2 * from_x + c],
            agg_full.at[2 * from_x + c],
            f_send.at[from_x],
            f_recv.at[from_x],
            (dp, 2 * x + 1 - c),
        )

    def f_wait_recv(from_x):
        remote(
            agg_full.at[2 * from_x + c],
            agg_full.at[2 * from_x + 1 - c],
            f_send.at[from_x],
            f_recv.at[from_x],
            (dp, 2 * x + 1 - c),
        ).wait_recv()

    def forward(step):
        from_x = lax.rem(x + nx - served(step), nx)
        a_wait_recv(from_x)
        f_copy(from_x).start()

    def aggregate(step, k, chip):
        b = 2 * chip + k
        count = tcnt[b]
        links = [mask_v[step, k, s].astype(f32).astype(bf16) for s in range(maxt)]
        picks = [jnp.where(s < count, srcx[tix[b, s]], jnp.zeros((), bf16)) for s in range(maxt)]
        total = jnp.dot(
            jnp.concatenate(links, axis=1), jnp.concatenate(picks, axis=0), preferred_element_type=f32
        )
        total = total.T
        return (total[:width] / jnp.maximum(total[width : width + 1], 1.0)).astype(bf16)

    def chip_step(step):
        chip = lax.rem(x + served(step), nx)
        mask_copy(step).wait()

        @pl.when(step + AHEAD < nx)
        def _():
            mask_copy(step + AHEAD).start()

        for k in (0, 1):
            agg_send[step, :, k * TILE : (k + 1) * TILE] = aggregate(step, k, chip)

        @pl.when(step == 0)
        def _():
            pl.semaphore_wait(barrier, 2 * nx - 1 + 4 * (n - 1))
            send_w1()
            cot_copy().start()

        @pl.when(step == min(2, nx - 1))
        def _():
            send_w2()

        @pl.when(step < nx - 1)
        def _():
            a_copy(step, chip).start()

        @pl.when(step >= 2)
        def _():
            forward(step - 2)

    each(nx, chip_step)
    agg_full[2 * x + c] = agg_send[nx - 1]
    f_copy(x).start()
    if nx >= 2:
        forward(jnp.int32(nx - 2))

    cot_x[c] = cot_own[:, pl.ds(pl.multiple_of(c * 2 * TILE, TILE), 2 * TILE)]
    remote(cot_own.at[:, pl.ds(0, 2 * TILE)], cot_x.at[1 - c], cx_send, cx_recv, (dp, 2 * x + 1 - c)).wait_recv()
    for k in (0, 1):
        cot_t[:, k * TILE : (k + 1) * TILE] = cot_x[k].astype(f32).T
    for ab in (0, 1):
        others(ab, functools.partial(w2_wait_recv, ab))
        w_t[ab * TILE : (ab + 1) * TILE, :] = w_ab[ab].reshape(nx * TILE, TILE).T

    each(nx, f_wait_recv)
    agg = agg_full[...].reshape(nx * TILE, 2 * TILE)
    zt = jnp.dot(w_t[...], agg, preferred_element_type=f32)
    sig = jax.nn.sigmoid(zt)
    hid_t = zt * sig
    dzt = (cot_t[...] * sig * (1.0 + zt * (1.0 - sig))).astype(bf16)
    part = lax.dot_general(agg, dzt, (((1,), (1,)), ((), ())), preferred_element_type=f32).astype(bf16)
    for ab in (0, 1):
        block = part[:, ab * TILE : (ab + 1) * TILE].reshape(nx, n, rows, TILE)
        for i in range(n):
            p1_send[ab, i] = block[:, i]

    def p1_copy(ab, i):
        return remote(
            p1_send.at[ab, i], p1_recv.at[ab, place[ab]], p1_ss.at[ab, i], p1_rs.at[ab, place[ab]], (at(ab, i), feat)
        )

    def p1_wait(ab, i):
        remote(
            p1_send.at[ab, i], p1_recv.at[ab, i], p1_ss.at[ab, i], p1_rs.at[ab, i], (at(ab, i), feat)
        ).wait_recv()

    for ab in (0, 1):
        others(ab, lambda i: p1_copy(ab, i).start())

    for k in (0, 1):
        hid_buf[k] = hid_t[:, k * TILE : (k + 1) * TILE].T.astype(bf16)
    hid_copy = remote(hid_buf.at[1 - c], hid_rx, h_send, h_recv, (dp, 2 * x + 1 - c))
    hid_copy.start()
    hid_out[:, pl.ds(pl.multiple_of(c * 2 * TILE, TILE), 2 * TILE)] = hid_buf[c]

    for ab in (0, 1):
        p1_recv[ab, place[ab]] = p1_send[ab, place[ab]]
        others(ab, functools.partial(p1_wait, ab))
        p2_send[:, ab] = jnp.sum(p1_recv[ab].astype(f32), axis=0).astype(bf16)

    def p2_copy(i):
        return remote(p2_send.at[i], p2_recv.at[x], p2_ss.at[i], p2_rs.at[x], (dp, 2 * i + c))

    def p2_wait(i):
        remote(p2_send.at[i], p2_recv.at[i], p2_ss.at[i], p2_rs.at[i], (dp, 2 * i + c)).wait_recv()

    def others_x(body):
        each(nx - 1, lambda i: body(lax.rem(x + 1 + i, nx)))

    others_x(lambda i: p2_copy(i).start())
    p2_recv[x] = p2_send[x]
    others_x(p2_wait)
    p3_send[...] = jnp.sum(p2_recv[...].astype(f32), axis=0)

    def p3_copy(ab, i):
        return remote(
            p3_send.at[ab], p3_recv.at[ab, place[1 - ab]], p3_ss.at[ab, i], p3_rs.at[ab, place[1 - ab]], (at(1 - ab, i), feat)
        )

    def p3_wait(ab, i):
        remote(
            p3_send.at[ab], p3_recv.at[ab, i], p3_ss.at[ab, i], p3_rs.at[ab, i], (at(1 - ab, i), feat)
        ).wait_recv()

    for ab in (0, 1):
        others(1 - ab, lambda i: p3_copy(ab, i).start())
    for ab in (0, 1):
        p3_recv[ab, place[1 - ab]] = p3_send[ab]
        others(1 - ab, functools.partial(p3_wait, ab))
        res[ab] = jnp.sum(p3_recv[ab], axis=0)

    def wg_at(ab, chunk, core):
        return wg_acc.at[chunk, :, pl.ds(pl.multiple_of(2 * TILE * core + TILE * ab, TILE), TILE)]

    def p4_copy(ab, i):
        return remote(
            res.at[ab],
            wg_at(ab, lax.rem(place[ab], half), c),
            p4_ss.at[ab, i],
            p4_rs.at[ab, lax.rem(place[ab], half), c],
            (at(ab, i), 2 * x + lax.div(place[ab], half)),
        )

    def p4_self(ab, i):
        return jnp.logical_and(i == place[ab], c == lax.div(place[ab], half))

    def p4_go(ab, start):
        def go(i):
            @pl.when(jnp.logical_not(p4_self(ab, i)))
            def _():
                copy = p4_copy(ab, i)
                copy.start() if start else copy.wait_send()

        each(n, go)

    for ab in (0, 1):
        p4_go(ab, True)

        @pl.when(c == lax.div(place[ab], half))
        def _():
            wg_acc[lax.rem(place[ab], half), :, pl.ds(pl.multiple_of(2 * TILE * c + TILE * ab, TILE), TILE)] = res[ab]

    hid_copy.wait()
    hid_out[:, pl.ds(pl.multiple_of((1 - c) * 2 * TILE, TILE), 2 * TILE)] = hid_rx[...]

    for ab in (0, 1):
        @pl.when(c == lax.div(place[ab], half))
        def _():
            for to_c in (0, 1):
                def gone(to_x):
                    @pl.when(jnp.logical_not(jnp.logical_and(to_x == x, to_c == c)))
                    def _():
                        w1_copy(ab, to_x, to_c).wait_send()

                each(nx, gone)
        others(ab, lambda i: w2_copy(ab, i).wait_send())
        others(ab, lambda i: p1_copy(ab, i).wait_send())
        others(1 - ab, lambda i: p3_copy(ab, i).wait_send())
        p4_go(ab, False)
    cot_copy().wait_send()
    each(nx - 1, lambda i: a_copy(i, jnp.int32(0)).wait_send())
    each(nx, lambda i: f_copy(i).wait_send())
    others_x(lambda i: p2_copy(i).wait_send())

    for ab in (0, 1):
        for core in (0, 1):
            def landed(chunk):
                own = jnp.logical_and(c == core, c * half + chunk == place[ab])

                @pl.when(jnp.logical_not(own))
                def _():
                    remote(
                        res.at[ab], wg_at(ab, chunk, core), p4_ss.at[ab, 0], p4_rs.at[ab, chunk, core], (dp, feat)
                    ).wait_recv()

            each(half, landed)
    wg_out[...] = wg_acc[...].reshape(wg_out.shape)


def solution(mesh):
    nx = mesh.shape["feat"] // 2
    n = round(mesh.shape["dp"] ** 0.5)

    def shards(source_feat, weight, tile_index, tile_count, tile_mask, cotangent):
        nblk, maxt, tile, _ = tile_mask.shape
        width = source_feat.shape[1]
        hid = weight.shape[1]
        rows = TILE // n
        half = n // 2
        bf16, f32 = jnp.bfloat16, jnp.float32
        dma = lambda *shape: pltpu.SemaphoreType.DMA(shape)
        vm = pltpu.VMEM
        nsrc = source_feat.shape[0] // tile
        anyspec = pl.BlockSpec(memory_space=pl.ANY)
        smem = pl.BlockSpec(memory_space=pltpu.SMEM)
        vmem = pl.BlockSpec(memory_space=pltpu.VMEM)
        hidden, weight_grad = pl.pallas_call(
            functools.partial(kernel, nx, n, maxt, width),
            out_shape=(
                jax.ShapeDtypeStruct((tile, hid), bf16),
                jax.ShapeDtypeStruct((width, hid), f32),
            ),
            in_specs=[smem, smem, anyspec, anyspec, anyspec, anyspec],
            out_specs=(vmem, vmem),
            scratch_shapes=[
                vm((nsrc, tile, width), bf16),
                vm((nsrc, tile, TILE), bf16),
                vm((nx, 2, maxt, tile, tile), jnp.int32),
                vm((half, rows, hid), bf16),
                vm((tile, hid), bf16),
                vm((2, tile, 2 * TILE), bf16),
                vm((2 * TILE, 2 * tile), f32),
                vm((2, nx, n, rows, TILE), bf16),
                vm((2 * TILE, nx * TILE), bf16),
                vm((nx, width, 2 * tile), bf16),
                vm((2 * nx, width, 2 * tile), bf16),
                vm((2, tile, 2 * TILE), bf16),
                vm((tile, 2 * TILE), bf16),
                vm((2, n, nx, rows, TILE), bf16),
                vm((2, n, nx, rows, TILE), bf16),
                vm((nx, 2, rows, TILE), bf16),
                vm((nx, 2, rows, TILE), bf16),
                vm((2, rows, TILE), f32),
                vm((2, n, rows, TILE), f32),
                vm((2, rows, TILE), f32),
                vm((half, rows, hid), f32),
                dma(), dma(nx), dma(), dma(),
                dma(), dma(),
                dma(2, 2, nx), dma(2, nx),
                dma(2, n), dma(2, n),
                dma(nx), dma(nx),
                dma(nx), dma(nx),
                dma(2, n), dma(2, n),
                dma(nx), dma(nx),
                dma(2, n), dma(2, n),
                dma(2, n), dma(2, half, 2),
                dma(), dma(),
            ],
            compiler_params=pltpu.CompilerParams(
                collective_id=0, has_side_effects=True, vmem_limit_bytes=40 * 1024 * 1024
            ),
        )(
            tile_index,
            tile_count,
            source_feat.reshape(nsrc, tile, width),
            weight.reshape(half, rows, hid),
            tile_mask,
            cotangent,
        )
        return hidden, weight_grad

    in_specs = (
        P("dp", "feat"),
        P("feat", None),
        P("dp", None),
        P("dp"),
        P("dp", None, None, None),
        P(("dp", "feat"), None),
    )
    out_specs = (P(("dp", "feat"), None), P("feat", None))
    return jax.shard_map(shards, mesh=mesh, in_specs=in_specs, out_specs=out_specs, check_vma=False)
```

time: 328 us -> 81 us (0.25); the launches traced: 324 us -> 80.7 us
  waiting for transfers between devices: 287 us -> 0 us
  Pallas kernels: 0 us -> 70.2 us
  between operations: 13.8 us -> 0.66 us
  matrix products: 11.1 us -> 0 us
  other arithmetic: 8.09 us -> 0 us
  local copies, waits for them, and re-layouts: 4.26 us -> 9.87 us
    psum x1 -> x0, waiting for transfers between devices: 161 us -> none  [shards(): weight_grad = lax.psum(piece, 'dp')]
    reduce_scatter x1 -> x0, waiting for transfers between devices: 79.5 us -> none  [shards(): lax.psum_scatter(jnp.dot(agg, weight, preferred_element_type=jnp.float32)...]
    pallas_call x0 -> x1, Pallas kernels: none -> 70.2 us  [shards(): pl.pallas_call(functools.partial(kernel, nx, n, maxt, width), out_shape=(...]
    all_gather x1 -> x0, waiting for transfers between devices: 46.3 us -> none  [shards(): slope_all = lax.all_gather(slope, 'feat', axis=0, tiled=True)]
    dot_general x3 -> x0, matrix products: 11.1 us -> none  [the longest x1 5.66 us: shards(): jnp.einsum('bsij,bsjf->bif', links.astype(jnp.bfloat16), picked, preferre...]
    unnamed x7 -> x12, local copies, waits for them, and re-layouts: 1.59 us -> 9.87 us
    reduce_sum x1 -> x0, other arithmetic: 4.13 us -> none  [shards(): degree = jnp.maximum(jnp.sum(links, axis=(1, 3)), 1).astype(jnp.float32)]
  transfers between devices with their start and end apart: 3 -> 0, of which waited for: 3 -> 0; matrix products, arithmetic and copies ran while one was open for 0% -> 0% of each run, Pallas kernels for 0% -> 0%
where the time goes in v1:
time: 81 us; the launch traced here: 80.7 us
  Pallas kernels  70.2 us (87%)
  local copies, waits for them, and re-layouts  9.87 us (12%)
    pallas_call x1, Pallas kernels, shards(): pl.pallas_call(functools.partial(kernel, nx, n, maxt, width), out_shape=(...  70.2 us
    unnamed x12, local copies, waits for them, and re-layouts  9.87 us

profile of v1, /device:TPU:1, one launch (start us, length us, event | category | flops | bytes accessed | tf_op | source)
XLA Modules:
  0.0 80.7 jit_solution(570563965120210406)
XLA Ops:
  0.6 0.8 copy.9.tix
  1.4 2.0 %copy.8 = bf16[8192,64]{1,0:T(8,128)(2,1)S(1)} copy(bf16[8192,64]{0,1:T(8,128)(2,1)} %param.6) | data formatting | bytes 2097152 | tf_op args[0]
  3.4 0.0 copy-start
  3.4 3.4 %copy-done = s32[16,8,128,128]{3,2,1,0:T(8,128)S(1)} copy-done((s32[16,8,128,128]{3,2,1,0:T(8,128)S(1)}, s32[16,8,128,128]{3,2,1,0:T(8,128)}, u32[]{:S(2)}) %copy-start) | copy-done | bytes 8388632
  6.8 0.0 copy-start.1
  6.8 0.9 %copy-done.1 = bf16[128,512]{1,0:T(8,128)(2,1)S(1)} copy-done((bf16[128,512]{1,0:T(8,128)(2,1)S(1)}, bf16[128,512]{1,0:T(8,128)(2,1)}, u32[]{:S(2)}) %copy-start.1) | copy-done | bytes 131096
  7.7 0.0 copy-start.2
  7.7 0.8 %copy-done.2 = bf16[64,512]{1,0:T(8,128)(2,1)S(1)} copy-done((bf16[64,512]{1,0:T(8,128)(2,1)S(1)}, bf16[64,512]{1,0:T(8,128)(2,1)}, u32[]{:S(2)}) %copy-start.2) | copy-done | bytes 65560
  8.5 0.0 copy-start.3
  8.5 0.7 copy-done.3
  9.2 70.2 %shard_map.77 = (bf16[128,512]{1,0:T(8,128)(2,1)S(1)}, f32[64,512]{1,0:T(8,128)S(1)}) custom-call(s32[16,8]{1,0:T(8,128)S(1)} %copy.9.tix, s32[16]{0:T(128)S(1)} %copy-done.3, bf16[64,128,64]{2,1,0:T(8,128)(2,1)S(1)} %bitcast.2, bf16[4,16,512]{2,1,0:T(8,128)(2,1)S(1)} %bitcast.3, s32[16,8,128,128]{3,2,1,0:T(8,128)S(1)} %copy-done, bf16[128,512]{1,0:T(8,128)(2,1)S(1)} %copy-done.1), custom_call_target="tpu_custom_call" | custom-call | tf_op jit(solution)/shard_map/pallas_call | solution.py:407
  79.4 0.7 copy.12
  80.0 0.7 copy.13
Async XLA Ops:
  3.4 3.4 %copy-start = (s32[16,8,128,128]{3,2,1,0:T(8,128)S(1)}, s32[16,8,128,128]{3,2,1,0:T(8,128)}, u32[]{:S(2)}) copy-start(s32[16,8,128,128]{3,2,1,0:T(8,128)} %mask.1) | copy-start | bytes 25165828
  6.8 0.9 %copy-start.1 = (bf16[128,512]{1,0:T(8,128)(2,1)S(1)}, bf16[128,512]{1,0:T(8,128)(2,1)}, u32[]{:S(2)}) copy-start(bf16[128,512]{1,0:T(8,128)(2,1)} %cot.1) | copy-start | bytes 393220
  7.7 0.8 %copy-start.2 = (bf16[64,512]{1,0:T(8,128)(2,1)S(1)}, bf16[64,512]{1,0:T(8,128)(2,1)}, u32[]{:S(2)}) copy-start(bf16[64,512]{1,0:T(8,128)(2,1)} %param.7) | copy-start | bytes 196612
  8.5 0.7 copy-start.3

commit v2 on v1

v2 whole, which is shorter than its diff:
```python
import functools

import jax
import jax.numpy as jnp
from jax import lax
from jax.experimental import pallas as pl
from jax.experimental.pallas import tpu as pltpu
from jax.sharding import PartitionSpec as P

MESH = pl.DeviceIdType.MESH
TILE = 128


def around(n):
    return sorted(range(1, n), key=lambda k: (-min(k, n - k), -k))


def slots(n):
    return [0] + around(n)[::-1]


def kernel(
    nx, n, maxt, width, tix_h, tcnt_h, src, weight, mask, cot, hid_out, wg_out,
    tix, tcnt, src_v, src_x, mask_v, w_own, cot_own, cot_x, cot_t, w_ab, w_t, agg_send, agg_full,
    hid_buf, hid_rx, p1_send, p1_recv, p2_send, p2_recv, p3_send, p3_recv, res, wg_acc,
    ix_sem, src_sem, mask_sem, w_sem, cot_sem, cx_send, cx_recv, wd_send, wd_recv, w1_send, w1_recv, w2_send, w2_recv,
    a_send, a_recv, f_send, f_recv, p1_ss, p1_rs, p2_ss, p2_rs, p3_ss, p3_rs, p4_ss, p4_rs, h_send, h_recv,
):
    dp = lax.axis_index("dp")
    feat = lax.axis_index("feat")
    y, z = lax.div(dp, n), lax.rem(dp, n)
    x, c = lax.div(feat, 2), lax.rem(feat, 2)
    half = n // 2
    rows = TILE // n
    rel = slots(nx)
    near = min(3, nx)
    far = [(a, b) for a, b in ((near, min(near + 2, nx)), (near + 2, nx)) if a < b]
    place = (y, z)
    f32, bf16 = jnp.float32, jnp.bfloat16

    def at(ab, i):
        return i * n + z if ab == 0 else y * n + i

    def remote(source, target, ssem, rsem, where):
        return pltpu.make_async_remote_copy(
            src_ref=source, dst_ref=target, send_sem=ssem, recv_sem=rsem, device_id=where, device_id_type=MESH
        )

    def each(count, body):
        def step(i, carry):
            body(i)
            return carry

        lax.fori_loop(0, count, step, 0)

    def served(step):
        off = jnp.where(lax.rem(step, 2) == 1, lax.div(nx - 1 - step, 2), nx // 2 + lax.div(step, 2))
        return off

    def mask_copy(step):
        chip = lax.rem(x + served(step), nx)
        return pltpu.make_async_copy(mask.at[pl.ds(2 * chip, 2)], mask_v.at[step], mask_sem.at[step])

    barrier = pltpu.get_barrier_semaphore()

    def greet(where):
        pl.semaphore_signal(barrier, inc=1, device_id=where, device_id_type=MESH)

    for off in around(nx):
        for core in (0, 1):
            greet((dp, 2 * lax.rem(x + off, nx) + core))
    for off in around(n):
        for ab in (0, 1):
            for core in (0, 1):
                greet((at(ab, lax.rem(place[ab] + off, n)), 2 * x + core))
    greet((dp, 2 * x + 1 - c))

    get_ix = [pltpu.make_async_copy(a, b, ix_sem.at[i]) for i, (a, b) in enumerate(((tix_h, tix), (tcnt_h, tcnt)))]
    for copy in get_ix:
        copy.start()
    get_src = pltpu.make_async_copy(src, src_v, src_sem)
    get_src.start()
    get_w = pltpu.make_async_copy(weight, w_own, w_sem)
    get_w.start()
    get_cot = pltpu.make_async_copy(cot, cot_own, cot_sem)
    get_cot.start()
    for k in range(nx):
        mask_copy(jnp.int32(k)).start()

    def w_part(ab, to_c):
        return pl.ds(pl.multiple_of(2 * TILE * to_c + TILE * ab, TILE), TILE)

    def chip_at(steps):
        return lax.rem(x + nx + steps, nx)

    def wd_copy(ab, slot, to_c):
        return remote(
            w_own.at[:, :, w_part(ab, to_c)],
            w_ab.at[ab, slot, pl.ds(half * c, half)],
            wd_send.at[ab, slot, to_c],
            wd_recv.at[ab, slot, c],
            (dp, 2 * chip_at(-rel[slot]) + to_c),
        )

    def wd_wait_recv(ab, slot, from_c):
        remote(
            w_own.at[:, :, pl.ds(0, TILE)],
            w_ab.at[ab, slot, pl.ds(half * from_c, half)],
            wd_send.at[ab, slot, 0],
            wd_recv.at[ab, slot, from_c],
            (dp, feat),
        ).wait_recv()

    def w1_copy(ab, slot, to_c):
        return remote(
            w_own.at[lax.rem(place[ab], half), :, w_part(ab, to_c)],
            w_ab.at[ab, slot, place[ab]],
            w1_send.at[ab, slot, to_c],
            w1_recv.at[ab, slot],
            (dp, 2 * chip_at(-rel[slot]) + to_c),
        )

    def w1_all(body):
        for ab in (0, 1):
            @pl.when(c == lax.div(place[ab], half))
            def _():
                for slot in reversed(range(near, nx)):
                    for to_c in (0, 1):
                        body(w1_copy(ab, slot, to_c))

    def wd_all(body):
        for ab in (0, 1):
            body(wd_copy(ab, 0, 1 - c))
            for slot in range(1, near):
                for to_c in (0, 1):
                    body(wd_copy(ab, slot, to_c))

    def w2_copy(ab, group, i):
        piece = w_ab.at[ab, far[group][0] : far[group][1], place[ab]]
        return remote(piece, piece, w2_send.at[ab, group, i], w2_recv.at[ab, group, place[ab]], (at(ab, i), feat))

    def w2_wait_recv(ab, group, i):
        remote(
            w_ab.at[ab, far[group][0] : far[group][1], place[ab]],
            w_ab.at[ab, far[group][0] : far[group][1], i],
            w2_send.at[ab, group, i],
            w2_recv.at[ab, group, i],
            (at(ab, i), feat),
        ).wait_recv()

    def others(ab, body):
        for off in around(n):
            body(lax.rem(place[ab] + off, n))

    def send_w2(group):
        for ab in (0, 1):
            for slot in range(*far[group]):
                remote(
                    w_own.at[0, :, pl.ds(0, TILE)],
                    w_ab.at[ab, slot, place[ab]],
                    w1_send.at[ab, slot, 0],
                    w1_recv.at[ab, slot],
                    (dp, feat),
                ).wait_recv()
            others(ab, lambda i, ab=ab: w2_copy(ab, group, i).start())

    def turn_w(first, last):
        for ab in (0, 1):
            for slot in range(first, last):
                w_t[ab * TILE : (ab + 1) * TILE, slot * TILE : (slot + 1) * TILE] = w_ab[ab, slot].reshape(TILE, TILE).T

    def cot_copy():
        return remote(
            cot_own.at[:, pl.ds(pl.multiple_of((1 - c) * 2 * TILE, TILE), 2 * TILE)],
            cot_x.at[c],
            cx_send,
            cx_recv,
            (dp, 2 * x + 1 - c),
        )

    def a_copy(step, to_x):
        slot = nx - 1 - step
        return remote(agg_send.at[step], agg_full.at[2 * slot + c], a_send.at[step], a_recv.at[slot], (dp, 2 * to_x + c))

    def f_copy(slot):
        return remote(
            agg_full.at[2 * slot + c],
            agg_full.at[2 * slot + c],
            f_send.at[slot],
            f_recv.at[slot],
            (dp, 2 * x + 1 - c),
        )

    def f_wait_recv(slot):
        remote(
            agg_full.at[2 * slot + c],
            agg_full.at[2 * slot + 1 - c],
            f_send.at[slot],
            f_recv.at[slot],
            (dp, 2 * x + 1 - c),
        ).wait_recv()

    def forward(step):
        slot = nx - 1 - step
        remote(agg_send.at[0], agg_full.at[2 * slot + c], a_send.at[0], a_recv.at[slot], (dp, feat)).wait_recv()
        f_copy(slot).start()

    def aggregate(step, k, chip):
        b = 2 * chip + k
        count = tcnt[0, b]
        links, picks = [], []
        for s in range(maxt):
            links.append(mask_v[step, k, s].astype(f32).astype(bf16))
            picks.append(jnp.where(s < count, src_x[tix[s, b]], jnp.zeros((), bf16)))
        total = lax.dot_general(
            jnp.concatenate(picks, axis=1),
            jnp.concatenate(links, axis=1),
            (((1,), (1,)), ((), ())),
            preferred_element_type=f32,
        )
        return (total[:width] / jnp.maximum(total[width : width + 1], 1.0)).astype(bf16)

    def chip_step(step):
        chip = lax.rem(x + served(step), nx)
        mask_copy(step).wait()
        for k in (0, 1):
            agg_send[step, :, k * TILE : (k + 1) * TILE] = aggregate(step, k, chip)

        @pl.when(step < nx - 1)
        def _():
            a_copy(step, chip).start()

    get_w.wait()
    pl.semaphore_wait(barrier, 2 * nx - 1 + 4 * (n - 1))
    w1_all(lambda copy: copy.start())
    wd_all(lambda copy: copy.start())
    get_cot.wait()
    cot_copy().start()
    for copy in get_ix:
        copy.wait()
    get_src.wait()
    ones = jnp.ones((16, TILE), bf16)
    for i in range(src_x.shape[0]):
        src_x[i] = jnp.concatenate([src_v[:, i * TILE : (i + 1) * TILE], ones], axis=0)
    each(nx, chip_step)
    agg_full[c] = agg_send[nx - 1]
    f_copy(0).start()

    for group in range(len(far)):
        send_w2(group)
    each(nx - 1, forward)

    cot_x[c] = cot_own[:, pl.ds(pl.multiple_of(c * 2 * TILE, TILE), 2 * TILE)]
    remote(cot_own.at[:, pl.ds(0, 2 * TILE)], cot_x.at[1 - c], cx_send, cx_recv, (dp, 2 * x + 1 - c)).wait_recv()
    for k in (0, 1):
        cot_t[:, k * TILE : (k + 1) * TILE] = cot_x[k].astype(f32).T
    for ab in (0, 1):
        w_ab[ab, 0, pl.ds(half * c, half)] = w_own[:, :, w_part(ab, c)]
        wd_wait_recv(ab, 0, 1 - c)
        for slot in range(1, near):
            for from_c in (0, 1):
                wd_wait_recv(ab, slot, from_c)
    turn_w(0, near)
    for group, (first, last) in enumerate(far):
        for ab in (0, 1):
            others(ab, functools.partial(w2_wait_recv, ab, group))
        turn_w(first, last)

    each(nx, f_wait_recv)
    agg = agg_full[...].reshape(nx * TILE, 2 * TILE)
    zt = jnp.dot(w_t[...], agg, preferred_element_type=f32)
    sig = jax.nn.sigmoid(zt)
    hid_t = zt * sig
    dzt = (cot_t[...] * sig * (1.0 + zt * (1.0 - sig))).astype(bf16)

    def p1_copy(ab, i):
        return remote(
            p1_send.at[ab, i], p1_recv.at[ab, place[ab]], p1_ss.at[ab, i], p1_rs.at[ab, place[ab]], (at(ab, i), feat)
        )

    def p1_wait(ab, i):
        remote(
            p1_send.at[ab, i], p1_recv.at[ab, i], p1_ss.at[ab, i], p1_rs.at[ab, i], (at(ab, i), feat)
        ).wait_recv()

    for ab in (0, 1):
        part = lax.dot_general(
            agg, dzt[ab * TILE : (ab + 1) * TILE], (((1,), (1,)), ((), ())), preferred_element_type=f32
        )
        block = part.astype(bf16).reshape(nx, n, rows, TILE)
        for i in range(n):
            p1_send[ab, i] = block[:, i]
        others(ab, lambda i, ab=ab: p1_copy(ab, i).start())

    for k in (0, 1):
        hid_buf[k] = hid_t[:, k * TILE : (k + 1) * TILE].T.astype(bf16)
    hid_copy = remote(hid_buf.at[1 - c], hid_rx, h_send, h_recv, (dp, 2 * x + 1 - c))
    hid_copy.start()
    hid_out[:, pl.ds(pl.multiple_of(c * 2 * TILE, TILE), 2 * TILE)] = hid_buf[c]

    for ab in (0, 1):
        p1_recv[ab, place[ab]] = p1_send[ab, place[ab]]
        others(ab, functools.partial(p1_wait, ab))
        p2_send[:, ab] = jnp.sum(p1_recv[ab].astype(f32), axis=0).astype(bf16)

    def p2_copy(slot):
        return remote(
            p2_send.at[slot], p2_recv.at[slot], p2_ss.at[slot], p2_rs.at[slot], (dp, 2 * chip_at(rel[slot]) + c)
        )

    for slot in reversed(range(1, nx)):
        p2_copy(slot).start()
    p2_recv[0] = p2_send[0]
    for slot in range(1, nx):
        p2_copy(slot).wait_recv()
    p3_send[...] = jnp.sum(p2_recv[...].astype(f32), axis=0)

    def p3_copy(ab, i):
        return remote(
            p3_send.at[ab], p3_recv.at[ab, place[1 - ab]], p3_ss.at[ab, i], p3_rs.at[ab, place[1 - ab]], (at(1 - ab, i), feat)
        )

    def p3_wait(ab, i):
        remote(
            p3_send.at[ab], p3_recv.at[ab, i], p3_ss.at[ab, i], p3_rs.at[ab, i], (at(1 - ab, i), feat)
        ).wait_recv()

    for ab in (0, 1):
        others(1 - ab, lambda i, ab=ab: p3_copy(ab, i).start())
    for ab in (0, 1):
        p3_recv[ab, place[1 - ab]] = p3_send[ab]
        others(1 - ab, functools.partial(p3_wait, ab))
        res[ab] = jnp.sum(p3_recv[ab], axis=0)

    def wg_at(ab, chunk, core):
        return wg_acc.at[chunk, :, pl.ds(pl.multiple_of(2 * TILE * core + TILE * ab, TILE), TILE)]

    def p4_copy(ab, i):
        return remote(
            res.at[ab],
            wg_at(ab, lax.rem(place[ab], half), c),
            p4_ss.at[ab, i],
            p4_rs.at[ab, lax.rem(place[ab], half), c],
            (at(ab, i), 2 * x + lax.div(place[ab], half)),
        )

    def p4_go(ab, start):
        def go(i):
            copy = p4_copy(ab, i)
            copy.start() if start else copy.wait_send()

        others(ab, go)

        @pl.when(c != lax.div(place[ab], half))
        def _():
            go(place[ab])

    for ab in (0, 1):
        p4_go(ab, True)

        @pl.when(c == lax.div(place[ab], half))
        def _():
            wg_acc[lax.rem(place[ab], half), :, pl.ds(pl.multiple_of(2 * TILE * c + TILE * ab, TILE), TILE)] = res[ab]

    hid_copy.wait()
    hid_out[:, pl.ds(pl.multiple_of((1 - c) * 2 * TILE, TILE), 2 * TILE)] = hid_rx[...]

    w1_all(lambda copy: copy.wait_send())
    wd_all(lambda copy: copy.wait_send())
    for ab in (0, 1):
        for group in range(len(far)):
            others(ab, lambda i: w2_copy(ab, group, i).wait_send())
        others(ab, lambda i: p1_copy(ab, i).wait_send())
        others(1 - ab, lambda i: p3_copy(ab, i).wait_send())
        p4_go(ab, False)
    cot_copy().wait_send()
    each(nx - 1, lambda i: a_copy(i, jnp.int32(0)).wait_send())
    each(nx, lambda i: f_copy(i).wait_send())
    for slot in range(1, nx):
        p2_copy(slot).wait_send()

    for ab in (0, 1):
        for core in (0, 1):
            def landed(chunk):
                own = jnp.logical_and(c == core, c * half + chunk == place[ab])

                @pl.when(jnp.logical_not(own))
                def _():
                    remote(
                        res.at[ab], wg_at(ab, chunk, core), p4_ss.at[ab, 0], p4_rs.at[ab, chunk, core], (dp, feat)
                    ).wait_recv()

            each(half, landed)
    wg_out[...] = wg_acc[...].reshape(wg_out.shape)


def solution(mesh):
    nx = mesh.shape["feat"] // 2
    n = round(mesh.shape["dp"] ** 0.5)

    def shards(source_feat, weight, tile_index, tile_count, tile_mask, cotangent):
        nblk, maxt, tile, _ = tile_mask.shape
        width = source_feat.shape[1]
        hid = weight.shape[1]
        rows = TILE // n
        half = n // 2
        bf16, f32 = jnp.bfloat16, jnp.float32
        dma = lambda *shape: pltpu.SemaphoreType.DMA(shape)
        vm = pltpu.VMEM
        hbm = pl.BlockSpec(memory_space=pltpu.HBM)
        vmem = pl.BlockSpec(memory_space=pltpu.VMEM)
        hidden, weight_grad = pl.pallas_call(
            functools.partial(kernel, nx, n, maxt, width),
            out_shape=(
                vm((tile, hid), bf16),
                vm((width, hid), f32),
            ),
            in_specs=[hbm] * 6,
            out_specs=(vmem, vmem),
            scratch_shapes=[
                pltpu.SMEM((maxt, nblk), jnp.int32),
                pltpu.SMEM((1, nblk), jnp.int32),
                vm((width, source_feat.shape[0]), bf16),
                vm((source_feat.shape[0] // tile, width + 16, tile), bf16),
                vm((nx, 2, maxt, tile, tile), jnp.int32),
                vm((half, rows, hid), bf16),
                vm((tile, hid), bf16),
                vm((2, tile, 2 * TILE), bf16),
                vm((2 * TILE, 2 * tile), f32),
                vm((2, nx, n, rows, TILE), bf16),
                vm((2 * TILE, nx * TILE), bf16),
                vm((nx, width, 2 * tile), bf16),
                vm((2 * nx, width, 2 * tile), bf16),
                vm((2, tile, 2 * TILE), bf16),
                vm((tile, 2 * TILE), bf16),
                vm((2, n, nx, rows, TILE), bf16),
                vm((2, n, nx, rows, TILE), bf16),
                vm((nx, 2, rows, TILE), bf16),
                vm((nx, 2, rows, TILE), bf16),
                vm((2, rows, TILE), f32),
                vm((2, n, rows, TILE), f32),
                vm((2, rows, TILE), f32),
                vm((half, rows, hid), f32),
                dma(2), dma(), dma(nx), dma(), dma(),
                dma(), dma(),
                dma(2, 3, 2), dma(2, 3, 2),
                dma(2, nx, 2), dma(2, nx),
                dma(2, 2, n), dma(2, 2, n),
                dma(nx), dma(nx),
                dma(nx), dma(nx),
                dma(2, n), dma(2, n),
                dma(nx), dma(nx),
                dma(2, n), dma(2, n),
                dma(2, n), dma(2, half, 2),
                dma(), dma(),
            ],
            compiler_params=pltpu.CompilerParams(
                collective_id=0, has_side_effects=True, vmem_limit_bytes=40 * 1024 * 1024
            ),
        )(
            *(
                pltpu.with_memory_space_constraint(a, pltpu.HBM)
                for a in (
                    tile_index.T,
                    tile_count.reshape(1, nblk),
                    source_feat.T,
                    weight.reshape(half, rows, hid),
                    tile_mask,
                    cotangent,
                )
            )
        )
        return hidden, weight_grad

    in_specs = (
        P("dp", "feat"),
        P("feat", None),
        P("dp", None),
        P("dp"),
        P("dp", None, None, None),
        P(("dp", "feat"), None),
    )
    out_specs = (P(("dp", "feat"), None), P("feat", None))
    return jax.shard_map(shards, mesh=mesh, in_specs=in_specs, out_specs=out_specs, check_vma=False)
```

time: 81 us -> 63.5 us (0.78)
  Pallas kernels: 70.2 us -> 61.4 us
  local copies, waits for them, and re-layouts: 9.87 us -> 1.31 us
    pallas_call x1, Pallas kernels: 70.2 us -> 61.4 us  [shards(): pl.pallas_call(functools.partial(kernel, nx, n, maxt, width), out_shape=(...]
    unnamed x12 -> x2, local copies, waits for them, and re-layouts: 9.87 us -> 1.31 us
where the time goes in v2:
time: 63.5 us; the launch traced here: 63.4 us
  Pallas kernels  61.4 us (97%)
  local copies, waits for them, and re-layouts  1.31 us (2%)
  between operations  0.64 us (1%)
    pallas_call x1, Pallas kernels, shards(): pl.pallas_call(functools.partial(kernel, nx, n, maxt, width), out_shape=(...  61.4 us
    unnamed x2, local copies, waits for them, and re-layouts  1.31 us

profile of v2, /device:TPU:1, one launch (start us, length us, event | category | flops | bytes accessed | tf_op | source)
XLA Modules:
  0.0 63.4 jit_solution(7475016810923391189)
XLA Ops:
  0.6 61.4 %shard_map.77 = (bf16[128,512]{1,0:T(8,128)(2,1)S(1)}, f32[64,512]{1,0:T(8,128)S(1)}) custom-call(s32[8,16]{1,0:T(8,128)} %bitcast.6, s32[1,16]{1,0:T(1,128)} %bitcast.7, bf16[64,8192]{1,0:T(8,128)(2,1)} %bitcast.4, bf16[4,16,512]{2,1,0:T(8,128)(2,1)} %bitcast.5, s32[16,8,128,128]{3,2,1,0:T(8,128)} %mask.1, bf16[128,512]{1,0:T(8,128)(2,1)} %cot.1), custom_call_target="tpu_custom_call" | custom-call | tf_op jit(solution)/shard_map/pallas_call | solution.py:412
  62.1 0.7 %copy.10 = bf16[128,512]{1,0:T(8,128)(2,1)} copy(bf16[128,512]{1,0:T(8,128)(2,1)S(1)} %get-tuple-element.2) | data formatting | bytes 262144
  62.7 0.7 %copy.11 = f32[64,512]{1,0:T(8,128)} copy(f32[64,512]{1,0:T(8,128)S(1)} %get-tuple-element.3) | data formatting | bytes 262144

commit v3 on v2

v3 whole, which is shorter than its diff:
```python
import functools

import jax
import jax.numpy as jnp
from jax import lax
from jax.experimental import pallas as pl
from jax.experimental.pallas import tpu as pltpu
from jax.sharding import PartitionSpec as P

MESH = pl.DeviceIdType.MESH
TILE = 128


def around(n):
    return sorted(range(1, n), key=lambda k: (-min(k, n - k), -k))


def slots(n):
    return [0] + around(n)[::-1]


def kernel(
    nx, n, maxt, width, tix_h, tcnt_h, src, weight, mask, cot, hid_out, wg_out,
    tix, tcnt, src_v, src_x, mask_v, w_own, cot_own, cot_x, cot_t, w_ab, w_t, agg_send, agg_full,
    hid_buf, hid_rx, p1x_send, p1x_recv, p1_send, p1_recv, p2x_send, p2x_recv, p2_send, p2_recv, p3_send, p3_recv, res, wg_acc,
    ix_sem, src_sem, mask_sem, w_sem, cot_sem, cx_send, cx_recv, wd_send, wd_recv, w1_send, w1_recv, w2_send, w2_recv,
    a_send, a_recv, f_send, f_recv, p1x_ss, p1x_rs, p1_ss, p1_rs, p2x_ss, p2x_rs, p2_ss, p2_rs, p3_ss, p3_rs, p4_ss, p4_rs, h_send, h_recv,
):
    dp = lax.axis_index("dp")
    feat = lax.axis_index("feat")
    y, z = lax.div(dp, n), lax.rem(dp, n)
    x, c = lax.div(feat, 2), lax.rem(feat, 2)
    half = n // 2
    rows = TILE // n
    rel = slots(nx)
    near = min(3, nx)
    far = [(a, b) for a, b in ((near, min(near + 2, nx)), (near + 2, nx)) if a < b]
    place = (y, z)
    f32, bf16 = jnp.float32, jnp.bfloat16

    def at(ab, i):
        return i * n + z if ab == 0 else y * n + i

    def remote(source, target, ssem, rsem, where):
        return pltpu.make_async_remote_copy(
            src_ref=source, dst_ref=target, send_sem=ssem, recv_sem=rsem, device_id=where, device_id_type=MESH
        )

    def arrived(ref, sem):
        remote(ref, ref, sem, sem, (dp, feat)).wait_recv()

    def left(ref, sem):
        remote(ref, ref, sem, sem, (dp, feat)).wait_send()

    def each(count, body):
        def step(i, carry):
            body(i)
            return carry

        lax.fori_loop(0, count, step, 0)

    def served(step):
        off = jnp.where(lax.rem(step, 2) == 1, lax.div(nx - 1 - step, 2), nx // 2 + lax.div(step, 2))
        return off

    def mask_copy(step):
        chip = lax.rem(x + served(step), nx)
        return pltpu.make_async_copy(mask.at[pl.ds(2 * chip, 2)], mask_v.at[step], mask_sem.at[step])

    barrier = pltpu.get_barrier_semaphore()

    def greet(where):
        pl.semaphore_signal(barrier, inc=1, device_id=where, device_id_type=MESH)

    for off in around(nx):
        for core in (0, 1):
            greet((dp, 2 * lax.rem(x + off, nx) + core))
    for off in around(n):
        for ab in (0, 1):
            for core in (0, 1):
                greet((at(ab, lax.rem(place[ab] + off, n)), 2 * x + core))
    greet((dp, 2 * x + 1 - c))

    get_ix = [pltpu.make_async_copy(a, b, ix_sem.at[i]) for i, (a, b) in enumerate(((tix_h, tix), (tcnt_h, tcnt)))]
    for copy in get_ix:
        copy.start()
    get_src = pltpu.make_async_copy(src, src_v, src_sem)
    get_src.start()
    get_w = pltpu.make_async_copy(weight, w_own, w_sem)
    get_w.start()
    get_cot = pltpu.make_async_copy(cot, cot_own, cot_sem)
    get_cot.start()
    for k in range(nx):
        mask_copy(jnp.int32(k)).start()

    def w_part(ab, to_c):
        return pl.ds(pl.multiple_of(2 * TILE * to_c + TILE * ab, TILE), TILE)

    def chip_at(steps):
        return lax.rem(x + nx + steps, nx)

    def wd_copy(ab, slot, to_c):
        return remote(
            w_own.at[:, :, w_part(ab, to_c)],
            w_ab.at[ab, slot, pl.ds(half * c, half)],
            wd_send.at[min(slot, 1)],
            wd_recv.at[min(slot, 1)],
            (dp, 2 * chip_at(-rel[slot]) + to_c),
        )

    def w1_copy(ab, slot, to_c):
        return remote(
            w_own.at[lax.rem(place[ab], half), :, w_part(ab, to_c)],
            w_ab.at[ab, slot, place[ab]],
            w1_send.at[ab],
            w1_recv.at[ab, [k for k, (a, b) in enumerate(far) if a <= slot < b][0]],
            (dp, 2 * chip_at(-rel[slot]) + to_c),
        )

    def sends_w1(ab):
        return c == lax.div(place[ab], half)

    def w2_copy(ab, group, i):
        piece = w_ab.at[ab, far[group][0] : far[group][1], place[ab]]
        return remote(piece, piece, w2_send.at[ab, group], w2_recv.at[ab, group], (at(ab, i), feat))

    def others(ab, body):
        for off in around(n):
            body(lax.rem(place[ab] + off, n))

    def send_w2(group):
        for ab in (0, 1):
            arrived(w_ab.at[ab, far[group][0] : far[group][1], place[ab]], w1_recv.at[ab, group])
            others(ab, lambda i, ab=ab: w2_copy(ab, group, i).start())

    def turn_w(first, last):
        for ab in (0, 1):
            for slot in range(first, last):
                w_t[ab * TILE : (ab + 1) * TILE, slot * TILE : (slot + 1) * TILE] = w_ab[ab, slot].reshape(TILE, TILE).T

    def cot_copy():
        return remote(
            cot_own.at[:, pl.ds(pl.multiple_of((1 - c) * 2 * TILE, TILE), 2 * TILE)],
            cot_x.at[c],
            cx_send,
            cx_recv,
            (dp, 2 * x + 1 - c),
        )

    def a_copy(step, to_x):
        slot = nx - 1 - step
        return remote(agg_send.at[step], agg_full.at[slot, c], a_send, a_recv.at[slot], (dp, 2 * to_x + c))

    def f_copy(slot):
        return remote(agg_full.at[slot, c], agg_full.at[slot, c], f_send, f_recv, (dp, 2 * x + 1 - c))

    def forward(step):
        slot = nx - 1 - step
        arrived(agg_full.at[slot, c], a_recv.at[slot])
        f_copy(slot).start()

    def aggregate(step, k, chip):
        b = 2 * chip + k
        count = tcnt[0, b]
        links, picks = [], []
        for s in range(maxt):
            links.append(mask_v[step, k, s].astype(f32).astype(bf16))
            picks.append(jnp.where(s < count, src_x[tix[s, b]], jnp.zeros((), bf16)))
        total = lax.dot_general(
            jnp.concatenate(picks, axis=1),
            jnp.concatenate(links, axis=1),
            (((1,), (1,)), ((), ())),
            preferred_element_type=f32,
        )
        return (total[:width] / jnp.maximum(total[width : width + 1], 1.0)).astype(bf16)

    def chip_step(step):
        chip = lax.rem(x + served(step), nx)
        mask_copy(step).wait()
        for k in (0, 1):
            agg_send[step, :, k * TILE : (k + 1) * TILE] = aggregate(step, k, chip)

        @pl.when(step < nx - 1)
        def _():
            a_copy(step, chip).start()

    get_w.wait()
    pl.semaphore_wait(barrier, 2 * nx - 1 + 4 * (n - 1))
    for ab in (0, 1):
        @pl.when(sends_w1(ab))
        def _():
            for slot in reversed(range(near, nx)):
                for to_c in (0, 1):
                    w1_copy(ab, slot, to_c).start()
    for slot in range(1, near):
        for ab in (0, 1):
            for to_c in (0, 1):
                wd_copy(ab, slot, to_c).start()
    for ab in (0, 1):
        wd_copy(ab, 0, 1 - c).start()
    get_cot.wait()
    cot_copy().start()
    for copy in get_ix:
        copy.wait()
    get_src.wait()
    ones = jnp.ones((16, TILE), bf16)
    for i in range(src_x.shape[0]):
        src_x[i] = jnp.concatenate([src_v[:, i * TILE : (i + 1) * TILE], ones], axis=0)
    each(nx, chip_step)
    agg_full[0, c] = agg_send[nx - 1]
    f_copy(0).start()

    for group in range(len(far)):
        send_w2(group)
    each(nx - 1, forward)

    cot_x[c] = cot_own[:, pl.ds(pl.multiple_of(c * 2 * TILE, TILE), 2 * TILE)]
    arrived(cot_x.at[1 - c], cx_recv)
    for k in (0, 1):
        cot_t[:, k * TILE : (k + 1) * TILE] = cot_x[k].astype(f32).T
    for ab in (0, 1):
        w_ab[ab, 0, pl.ds(half * c, half)] = w_own[:, :, w_part(ab, c)]
    arrived(w_ab.at[:, 0, pl.ds(half * (1 - c), half)], wd_recv.at[0])
    arrived(w_ab.at[:, 1:near], wd_recv.at[1])
    turn_w(0, near)
    for group, (first, last) in enumerate(far):
        for ab in (0, 1):
            arrived(w_ab.at[ab, first:last, 0 : n - 1], w2_recv.at[ab, group])
        turn_w(first, last)

    arrived(agg_full.at[:, 1 - c], f_recv)
    agg = agg_full[...].reshape(nx * TILE, 2 * TILE)
    zt = jnp.dot(w_t[...], agg, preferred_element_type=f32)
    sig = jax.nn.sigmoid(zt)
    hid_t = zt * sig
    dzt = (cot_t[...] * sig * (1.0 + zt * (1.0 - sig))).astype(bf16)

    turn = (0, 1, c)
    late = 1 - c
    r = TILE // 2 // n

    def spot(axis):
        return y + axis * (z - y)

    def to(axis, i):
        return i * n + z + axis * (y * n + i - i * n - z)

    def p1_copy(k, i):
        return remote(
            p1_send.at[k, i], p1_recv.at[k, spot(turn[k])], p1_ss.at[k], p1_rs.at[k], (to(turn[k], i), feat)
        )

    def p2x_copy(i):
        return remote(p2x_send.at[i], p2x_recv.at[spot(late)], p2x_ss, p2x_rs, (to(late, i), feat))

    def along(axis, body):
        for off in around(n):
            body(lax.rem(spot(axis) + off, n))

    def slot_copy(send, recv, ssem, rsem, slot):
        return remote(send.at[slot], recv.at[slot], ssem, rsem, (dp, 2 * chip_at(rel[slot]) + c))

    p1x_copy = functools.partial(slot_copy, p1x_send, p1x_recv, p1x_ss, p1x_rs)
    p2_copy = functools.partial(slot_copy, p2_send, p2_recv, p2_ss, p2_rs)

    for ab in (0, 1):
        part = lax.dot_general(
            agg, dzt[ab * TILE : (ab + 1) * TILE], (((1,), (1,)), ((), ())), preferred_element_type=f32
        ).reshape(nx, 2, n, r, TILE)
        for h in (0, 1):
            if ab + h == 0:
                p1x_send[...] = part[:, h].reshape(nx, TILE // 2, TILE).astype(bf16)
            else:
                for i in range(n):
                    p1_send[2 * ab + h - 1, i] = part[:, h, i].reshape(nx // 2, 2 * r, TILE).astype(bf16)
    for step in range(max(n, nx) - 1):
        if step < n - 1:
            for k in range(3):
                p1_copy(k, lax.rem(spot(turn[k]) + around(n)[step], n)).start()
        if step < nx - 1:
            p1x_copy(nx - 1 - step).start()

    for k in (0, 1):
        hid_buf[k] = hid_t[:, k * TILE : (k + 1) * TILE].T.astype(bf16)
    hid_copy = remote(hid_buf.at[1 - c], hid_rx, h_send, h_recv, (dp, 2 * x + 1 - c))
    hid_copy.start()
    hid_out[:, pl.ds(pl.multiple_of(c * 2 * TILE, TILE), 2 * TILE)] = hid_buf[c]

    for ab in (0, 1):
        if far:
            @pl.when(sends_w1(ab))
            def _():
                left(w_ab.at[ab, near:nx, 0:2], w1_send.at[ab])
        for group, (first, last) in enumerate(far):
            left(w_ab.at[ab, first:last, 0 : n - 1], w2_send.at[ab, group])
    left(w_ab.at[0, 0], wd_send.at[0])
    left(w_ab.at[:, 1:near], wd_send.at[1])
    left(cot_x.at[0], cx_send)
    left(agg_send.at[0 : nx - 1], a_send)
    left(agg_full.at[:, c], f_send)

    p1x_recv[0] = p1x_send[0]
    arrived(p1x_recv.at[1:nx], p1x_rs)
    p2x_send[...] = jnp.sum(p1x_recv[...].astype(f32), axis=0).reshape(n, r, TILE)
    along(late, lambda i: p2x_copy(i).start())
    for k in range(3):
        p1_recv[k, spot(turn[k])] = p1_send[k, spot(turn[k])]
        arrived(p1_recv.at[k, 0 : n - 1], p1_rs.at[k])
        p2_send[:, k] = jnp.sum(p1_recv[k].astype(f32), axis=0).reshape(nx, r, TILE)
    for slot in reversed(range(1, nx)):
        p2_copy(slot).start()
    left(p1x_send.at[1:nx], p1x_ss)
    for k in range(3):
        left(p1_send.at[k, 0 : n - 1], p1_ss.at[k])
    p2x_recv[spot(late)] = p2x_send[spot(late)]
    arrived(p2x_recv.at[0 : n - 1], p2x_rs)
    group0 = jnp.sum(p2x_recv[...], axis=0)
    p2_recv[0] = p2_send[0]
    arrived(p2_recv.at[1:nx], p2_rs)
    groups = jnp.sum(p2_recv[...], axis=0)

    for ab in (0, 1):
        p3_send[ab] = jnp.concatenate([groups[ab], jnp.where(c == ab, groups[2], group0)], axis=0).astype(bf16)

    def p3_copy(ab, i):
        return remote(p3_send.at[ab], p3_recv.at[ab, place[1 - ab]], p3_ss.at[ab], p3_rs.at[ab], (at(1 - ab, i), feat))

    for off in around(n):
        for ab in (0, 1):
            p3_copy(ab, lax.rem(place[1 - ab] + off, n)).start()
    left(p2x_send.at[0 : n - 1], p2x_ss)
    left(p2_send.at[1:nx], p2_ss)
    for ab in (0, 1):
        p3_recv[ab, place[1 - ab]] = p3_send[ab]
        arrived(p3_recv.at[ab, 0 : n - 1], p3_rs.at[ab])
        res[ab] = jnp.sum(p3_recv[ab].astype(f32), axis=0).reshape(2, r, TILE)

    def owner(ab, k):
        if k == 0:
            return 1 - ab, ab
        third = 1 - (c - ab) * (c - ab)
        return third, third

    def p4_copy(ab, k, i, sem):
        h, columns = owner(ab, k)
        return remote(
            res.at[ab, k], wg_acc.at[4 * place[ab] + 2 * c + columns], p4_ss.at[sem], p4_rs, (at(ab, i), 2 * x + h)
        )

    for off in around(n):
        for ab in (0, 1):
            for k in (0, 1):
                p4_copy(ab, k, lax.rem(place[ab] + off, n), 0).start()
    for ab in (0, 1):
        for k in (0, 1):
            @pl.when(owner(ab, k)[0] != c)
            def _():
                p4_copy(ab, k, place[ab], 1).start()

            @pl.when(owner(ab, k)[0] == c)
            def _():
                wg_acc[4 * place[ab] + 2 * c + owner(ab, k)[1]] = res[ab, k]

    hid_copy.wait()
    hid_out[:, pl.ds(pl.multiple_of((1 - c) * 2 * TILE, TILE), 2 * TILE)] = hid_rx[...]

    for ab in (0, 1):
        left(p3_recv.at[ab, 0 : n - 1], p3_ss.at[ab])
    left(wg_acc.at[0 : 4 * (n - 1)], p4_ss.at[0])
    left(res.at[0], p4_ss.at[1])

    arrived(wg_acc.at[0 : 4 * n - 2], p4_rs)
    for i in range(n):
        for block in range(4):
            wg_out[i * r : (i + 1) * r, block * TILE : (block + 1) * TILE] = wg_acc[4 * i + block]


def solution(mesh):
    nx = mesh.shape["feat"] // 2
    n = round(mesh.shape["dp"] ** 0.5)

    def shards(source_feat, weight, tile_index, tile_count, tile_mask, cotangent):
        nblk, maxt, tile, _ = tile_mask.shape
        width = source_feat.shape[1]
        hid = weight.shape[1]
        rows = TILE // n
        half = n // 2
        bf16, f32 = jnp.bfloat16, jnp.float32
        dma = lambda *shape: pltpu.SemaphoreType.DMA(shape)
        vm = pltpu.VMEM
        hbm = pl.BlockSpec(memory_space=pltpu.HBM)
        vmem = pl.BlockSpec(memory_space=pltpu.VMEM)
        hidden, weight_grad = pl.pallas_call(
            functools.partial(kernel, nx, n, maxt, width),
            out_shape=(
                vm((tile, hid), bf16),
                vm((width, hid), f32),
            ),
            in_specs=[hbm] * 6,
            out_specs=(vmem, vmem),
            scratch_shapes=[
                pltpu.SMEM((maxt, nblk), jnp.int32),
                pltpu.SMEM((1, nblk), jnp.int32),
                vm((width, source_feat.shape[0]), bf16),
                vm((source_feat.shape[0] // tile, width + 16, tile), bf16),
                vm((nx, 2, maxt, tile, tile), jnp.int32),
                vm((half, rows, hid), bf16),
                vm((tile, hid), bf16),
                vm((2, tile, 2 * TILE), bf16),
                vm((2 * TILE, 2 * tile), f32),
                vm((2, nx, n, rows, TILE), bf16),
                vm((2 * TILE, nx * TILE), bf16),
                vm((nx, width, 2 * tile), bf16),
                vm((nx, 2, width, 2 * tile), bf16),
                vm((2, tile, 2 * TILE), bf16),
                vm((tile, 2 * TILE), bf16),
                vm((nx, TILE // 2, TILE), bf16),
                vm((nx, TILE // 2, TILE), bf16),
                vm((3, n, nx // 2, rows, TILE), bf16),
                vm((3, n, nx // 2, rows, TILE), bf16),
                vm((n, rows // 2, TILE), f32),
                vm((n, rows // 2, TILE), f32),
                vm((nx, 3, rows // 2, TILE), f32),
                vm((nx, 3, rows // 2, TILE), f32),
                vm((2, rows, TILE), bf16),
                vm((2, n, rows, TILE), bf16),
                vm((2, 2, rows // 2, TILE), f32),
                vm((4 * n, rows // 2, TILE), f32),
                dma(2), dma(), dma(nx), dma(), dma(),
                dma(), dma(),
                dma(2), dma(2),
                dma(2), dma(2, 2),
                dma(2, 2), dma(2, 2),
                dma(), dma(nx),
                dma(), dma(),
                dma(), dma(),
                dma(3), dma(3),
                dma(), dma(),
                dma(), dma(),
                dma(2), dma(2),
                dma(2), dma(),
                dma(), dma(),
            ],
            compiler_params=pltpu.CompilerParams(
                collective_id=0, has_side_effects=True, vmem_limit_bytes=40 * 1024 * 1024
            ),
        )(
            *(
                pltpu.with_memory_space_constraint(a, pltpu.HBM)
                for a in (
                    tile_index.T,
                    tile_count.reshape(1, nblk),
                    source_feat.T,
                    weight.reshape(half, rows, hid),
                    tile_mask,
                    cotangent,
                )
            )
        )
        return hidden, weight_grad

    in_specs = (
        P("dp", "feat"),
        P("feat", None),
        P("dp", None),
        P("dp"),
        P("dp", None, None, None),
        P(("dp", "feat"), None),
    )
    out_specs = (P(("dp", "feat"), None), P("feat", None))
    return jax.shard_map(shards, mesh=mesh, in_specs=in_specs, out_specs=out_specs, check_vma=False)
```

time: 63.5 us -> 60.1 us (0.946)
  Pallas kernels: 61.4 us -> 58 us
    pallas_call x1, Pallas kernels: 61.4 us -> 58 us  [shards(): pl.pallas_call(functools.partial(kernel, nx, n, maxt, width), out_shape=(...]
where the time goes in v3:
time: 60.1 us; the launch traced here: 59.9 us
  Pallas kernels  58 us (97%)
  local copies, waits for them, and re-layouts  1.31 us (2%)
  between operations  0.64 us (1%)
    pallas_call x1, Pallas kernels, shards(): pl.pallas_call(functools.partial(kernel, nx, n, maxt, width), out_shape=(...  58 us
    unnamed x2, local copies, waits for them, and re-layouts  1.31 us

profile of v3, /device:TPU:1, one launch (start us, length us, event | category | flops | bytes accessed | tf_op | source)
XLA Modules:
  0.0 59.9 jit_solution(8141959735583763702)
XLA Ops:
  0.6 58.0 %shard_map.77 = (bf16[128,512]{1,0:T(8,128)(2,1)S(1)}, f32[64,512]{1,0:T(8,128)S(1)}) custom-call(s32[8,16]{1,0:T(8,128)} %bitcast.6, s32[1,16]{1,0:T(1,128)} %bitcast.7, bf16[64,8192]{1,0:T(8,128)(2,1)} %bitcast.4, bf16[4,16,512]{2,1,0:T(8,128)(2,1)} %bitcast.5, s32[16,8,128,128]{3,2,1,0:T(8,128)} %mask.1, bf16[128,512]{1,0:T(8,128)(2,1)} %cot.1), custom_call_target="tpu_custom_call" | custom-call | tf_op jit(solution)/shard_map/pallas_call | solution.py:393
  58.6 0.7 %copy.10 = bf16[128,512]{1,0:T(8,128)(2,1)} copy(bf16[128,512]{1,0:T(8,128)(2,1)S(1)} %get-tuple-element.2) | data formatting | bytes 262144
  59.3 0.7 %copy.11 = f32[64,512]{1,0:T(8,128)} copy(f32[64,512]{1,0:T(8,128)S(1)} %get-tuple-element.3) | data formatting | bytes 262144

commit v4 on v3

v4 whole, which is shorter than its diff:
```python
import functools

import jax
import jax.numpy as jnp
from jax import lax
from jax.experimental import pallas as pl
from jax.experimental.pallas import tpu as pltpu
from jax.sharding import PartitionSpec as P

MESH = pl.DeviceIdType.MESH
TILE = 128


def around(n):
    return sorted(range(1, n), key=lambda k: (-min(k, n - k), -k))


def slots(n):
    return [0] + around(n)[::-1]


def kernel(
    nx, n, maxt, width, tix_h, tcnt_h, src, weight, mask, cot, hid_out, wg_out,
    tix, tcnt, src_v, src_x, mask_v, w_own, cot_x, w_near, w_ab, agg_send, agg_full, z_send, z_recv,
    p1x_send, p1x_recv, pair_send, pair_recv, lone_send, lone_recv, p2x_send, p2x_recv, p2_send, p2_recv,
    p3_send, p3_recv, res, wg_acc,
    ix_sem, src_sem, mask_sem, w_sem, cot_sem, cx_send, cx_recv, wd_send, wd_recv, w1_send, w1_recv, w2_send, w2_recv,
    a_send, a_recv, z_ss, z_rs, p1x_ss, p1x_rs, pair_ss, pair_rs, lone_ss, lone_rs, p2x_ss, p2x_rs, p2_ss, p2_rs,
    p3_ss, p3_rs, p4_ss, p4_rs,
):
    dp = lax.axis_index("dp")
    feat = lax.axis_index("feat")
    y, z = lax.div(dp, n), lax.rem(dp, n)
    x, c = lax.div(feat, 2), lax.rem(feat, 2)
    half = n // 2
    rows = TILE // n
    rel = slots(nx)
    near = min(3, nx)
    far = [(a, b) for a, b in ((near, min(near + 2, nx)), (near + 2, nx)) if a < b]
    place = (y, z)
    f32, bf16 = jnp.float32, jnp.bfloat16

    def at(ab, i):
        return i * n + z if ab == 0 else y * n + i

    def spot(axis):
        return y + axis * (z - y)

    def to(axis, i):
        return i * n + z + axis * (y * n + i - i * n - z)

    def remote(source, target, ssem, rsem, where):
        return pltpu.make_async_remote_copy(
            src_ref=source, dst_ref=target, send_sem=ssem, recv_sem=rsem, device_id=where, device_id_type=MESH
        )

    def arrived(ref, sem):
        remote(ref, ref, sem, sem, (dp, feat)).wait_recv()

    def left(ref, sem):
        remote(ref, ref, sem, sem, (dp, feat)).wait_send()

    def each(count, body):
        def step(i, carry):
            body(i)
            return carry

        lax.fori_loop(0, count, step, 0)

    def served(step):
        off = jnp.where(lax.rem(step, 2) == 1, lax.div(nx - 1 - step, 2), nx // 2 + lax.div(step, 2))
        return off

    def mask_copy(step):
        chip = lax.rem(x + served(step), nx)
        return pltpu.make_async_copy(mask.at[pl.ds(2 * chip, 2)], mask_v.at[step], mask_sem.at[step])

    barrier = pltpu.get_barrier_semaphore()

    def greet(where):
        pl.semaphore_signal(barrier, inc=1, device_id=where, device_id_type=MESH)

    get_w = pltpu.make_async_copy(weight, w_own, w_sem)
    get_ix = [pltpu.make_async_copy(a, b, ix_sem.at[i]) for i, (a, b) in enumerate(((tix_h, tix), (tcnt_h, tcnt)))]
    get_src = pltpu.make_async_copy(src, src_v, src_sem)
    get_cot = pltpu.make_async_copy(cot, cot_x.at[c], cot_sem)
    for copy in (get_w, *get_ix, get_src):
        copy.start()
    for k in range(2):
        mask_copy(jnp.int32(k)).start()
    for off in around(nx):
        greet((dp, 2 * lax.rem(x + off, nx) + c))
    greet((dp, 2 * x + 1 - c))
    for off in around(n):
        for ab in (0, 1):
            greet((at(ab, lax.rem(place[ab] + off, n)), feat))
    for k in range(2, nx):
        mask_copy(jnp.int32(k)).start()
    get_cot.start()

    def chip_at(steps):
        return lax.rem(x + nx + steps, nx)

    def wd_copy(slot):
        return remote(w_own, w_near.at[slot], wd_send, wd_recv, (dp, 2 * chip_at(-rel[slot]) + c))

    def w1_copy(ab, slot):
        column = pl.multiple_of((2 * ab + lax.div(place[ab], half)) * TILE, TILE)
        return remote(
            w_own.at[lax.rem(place[ab], half), :, pl.ds(column, TILE)],
            w_ab.at[ab, slot, place[ab]],
            w1_send.at[ab],
            w1_recv.at[ab, [k for k, (a, b) in enumerate(far) if a <= slot < b][0]],
            (dp, 2 * chip_at(-rel[slot]) + c),
        )

    def w2_copy(ab, group, i):
        piece = w_ab.at[ab, far[group][0] : far[group][1], place[ab]]
        return remote(piece, piece, w2_send.at[ab, group], w2_recv.at[ab, group], (at(ab, i), feat))

    def others(ab, body):
        for off in around(n):
            body(lax.rem(place[ab] + off, n))

    def send_w2(group):
        for ab in (0, 1):
            arrived(w_ab.at[ab, far[group][0] : far[group][1], place[ab]], w1_recv.at[ab, group])
            others(ab, lambda i, ab=ab: w2_copy(ab, group, i).start())

    def cot_copy():
        return remote(cot_x.at[c], cot_x.at[c], cx_send, cx_recv, (dp, 2 * x + 1 - c))

    def a_copy(step, to_x):
        slot = nx - 1 - step
        return remote(agg_send.at[step], agg_full.at[slot], a_send, a_recv, (dp, 2 * to_x + c))

    def aggregate(step, k, chip):
        b = 2 * chip + k
        count = tcnt[0, b]
        links, picks = [], []
        for s in range(maxt):
            links.append(mask_v[step, k, s].astype(f32).astype(bf16))
            picks.append(jnp.where(s < count, src_x[tix[s, b]], jnp.zeros((), bf16)))
        total = lax.dot_general(
            jnp.concatenate(picks, axis=1),
            jnp.concatenate(links, axis=1),
            (((1,), (1,)), ((), ())),
            preferred_element_type=f32,
        )
        return (total[:width] / jnp.maximum(total[width : width + 1], 1.0)).astype(bf16)

    def chip_step(step):
        chip = lax.rem(x + served(step), nx)
        mask_copy(step).wait()
        for k in (0, 1):
            agg_send[step, :, k * TILE : (k + 1) * TILE] = aggregate(step, k, chip)

        @pl.when(step < nx - 1)
        def _():
            a_copy(step, chip).start()

    get_w.wait()
    pl.semaphore_wait(barrier, nx + 2 * (n - 1))
    for slot in reversed(range(near, nx)):
        for ab in (0, 1):
            w1_copy(ab, slot).start()
    for slot in range(1, near):
        wd_copy(slot).start()
    get_cot.wait()
    cot_copy().start()
    for copy in get_ix:
        copy.wait()
    get_src.wait()
    ones = jnp.ones((16, TILE), bf16)
    for i in range(src_x.shape[0]):
        src_x[i] = jnp.concatenate([src_v[:, i * TILE : (i + 1) * TILE], ones], axis=0)
    each(nx, chip_step)
    agg_full[0] = agg_send[nx - 1]

    for group in range(len(far)):
        send_w2(group)

    arrived(cot_x.at[1 - c], cx_recv)
    cot_all = cot_x[...].reshape(2 * TILE, 4 * TILE).astype(f32)
    w_near[0] = w_own[...]
    arrived(w_near.at[1:near], wd_recv)
    arrived(agg_full.at[1:nx], a_recv)
    agg = agg_full[...].reshape(nx * width, 2 * TILE)
    agg_t = agg.T
    pieces = [w_near[slot].reshape(width, 4 * TILE) for slot in range(near)]
    for group, (first, last) in enumerate(far):
        for ab in (0, 1):
            arrived(w_ab.at[ab, first:last, 0 : n - 1], w2_recv.at[ab, group])
        for slot in range(first, last):
            columns = [w_ab[ab, slot, k * half : (k + 1) * half] for ab in (0, 1) for k in (0, 1)]
            pieces.append(jnp.concatenate([piece.reshape(width, TILE) for piece in columns], axis=1))
    part = jnp.dot(agg_t, jnp.concatenate(pieces, axis=0), preferred_element_type=f32)
    z_send[...] = part.astype(bf16)
    z_copy = remote(z_send, z_recv, z_ss, z_rs, (dp, 2 * x + 1 - c))
    z_copy.start()
    z_copy.wait()
    zt = part + z_recv[...].astype(f32)
    sig = jax.nn.sigmoid(zt)
    dz = (cot_all * sig * (1.0 + zt * (1.0 - sig))).astype(bf16)
    hid = zt * sig

    r = TILE // 2 // n

    def pair_copy(i):
        return remote(pair_send.at[i], pair_recv.at[spot(c)], pair_ss, pair_rs, (to(c, i), feat))

    def lone_copy(i):
        return remote(lone_send.at[i], lone_recv.at[spot(1 - c)], lone_ss, lone_rs, (to(1 - c, i), feat))

    def p2x_copy(i):
        return remote(p2x_send.at[i], p2x_recv.at[spot(1 - c)], p2x_ss, p2x_rs, (to(1 - c, i), feat))

    def along(axis, body):
        for off in around(n):
            body(lax.rem(spot(axis) + off, n))

    def slot_copy(send, recv, ssem, rsem, slot):
        return remote(send.at[slot], recv.at[slot], ssem, rsem, (dp, 2 * chip_at(rel[slot]) + c))

    p1x_copy = functools.partial(slot_copy, p1x_send, p1x_recv, p1x_ss, p1x_rs)
    p2_copy = functools.partial(slot_copy, p2_send, p2_recv, p2_ss, p2_rs)

    for group in range(4):
        part = jnp.dot(agg, dz[:, group * TILE : (group + 1) * TILE], preferred_element_type=f32)
        if group == 0:
            p1x_send[...] = part.reshape(nx, width, TILE).astype(bf16)
            continue
        part = part.reshape(nx, n, r, TILE)
        for i in range(n):
            piece = part[:, i].reshape(nx // 2, 2 * r, TILE).astype(bf16)
            if group == 1:
                lone_send[i] = piece
            else:
                pair_send[i, group - 2] = piece
    for step in range(max(n, nx) - 1):
        if step < n - 1:
            pair_copy(lax.rem(spot(c) + around(n)[step], n)).start()
            lone_copy(lax.rem(spot(1 - c) + around(n)[step], n)).start()
        if step < nx - 1:
            p1x_copy(nx - 1 - step).start()

    hid_out[...] = jnp.where(c == 0, hid[:TILE], hid[TILE:]).astype(bf16)
    if far:
        for ab in (0, 1):
            left(w_ab.at[ab, near:nx, 0], w1_send.at[ab])
    for group, (first, last) in enumerate(far):
        for ab in (0, 1):
            left(w_ab.at[ab, first:last, 0 : n - 1], w2_send.at[ab, group])
    left(w_near.at[1:near], wd_send)
    left(cot_x.at[0], cx_send)
    left(agg_send.at[0 : nx - 1], a_send)

    p1x_recv[0] = p1x_send[0]
    arrived(p1x_recv.at[1:nx], p1x_rs)
    p2x_send[...] = jnp.sum(p1x_recv[...].astype(f32), axis=0).reshape(n, r, TILE)
    along(1 - c, lambda i: p2x_copy(i).start())
    lone_recv[spot(1 - c)] = lone_send[spot(1 - c)]
    arrived(lone_recv.at[0 : n - 1], lone_rs)
    p2_send[:, 2] = jnp.sum(lone_recv[...].astype(f32), axis=0).reshape(nx, r, TILE)
    pair_recv[spot(c)] = pair_send[spot(c)]
    arrived(pair_recv.at[0 : n - 1], pair_rs)
    for k in (0, 1):
        p2_send[:, k] = jnp.sum(pair_recv[:, k].astype(f32), axis=0).reshape(nx, r, TILE)
    for slot in reversed(range(1, nx)):
        p2_copy(slot).start()
    left(p1x_send.at[1:nx], p1x_ss)
    left(pair_send.at[0 : n - 1], pair_ss)
    left(lone_send.at[0 : n - 1], lone_ss)
    p2x_recv[spot(1 - c)] = p2x_send[spot(1 - c)]
    arrived(p2x_recv.at[0 : n - 1], p2x_rs)
    group0 = jnp.sum(p2x_recv[...], axis=0)
    p2_recv[0] = p2_send[0]
    arrived(p2_recv.at[1:nx], p2_rs)
    groups = jnp.sum(p2_recv[...], axis=0)

    cuts = (1 - c, c)
    pairs = ((group0, groups[2]), (groups[0], groups[1]))
    for q in (0, 1):
        p3_send[q] = jnp.concatenate(pairs[q], axis=0).astype(bf16)

    def p3_copy(q, i):
        axis = 1 - cuts[q]
        return remote(p3_send.at[q], p3_recv.at[q, spot(axis)], p3_ss.at[q], p3_rs.at[q], (to(axis, i), feat))

    for off in around(n):
        for q in (0, 1):
            p3_copy(q, lax.rem(spot(1 - cuts[q]) + off, n)).start()
    left(p2x_send.at[0 : n - 1], p2x_ss)
    left(p2_send.at[1:nx], p2_ss)
    for q in (0, 1):
        p3_recv[q, spot(1 - cuts[q])] = p3_send[q]
        arrived(p3_recv.at[q, 0 : n - 1], p3_rs.at[q])
        res[q] = jnp.sum(p3_recv[q].astype(f32), axis=0).reshape(2, r, TILE)

    def p4_copy(q, i):
        return remote(res.at[q], wg_acc.at[spot(cuts[q]), q], p4_ss.at[q], p4_rs.at[q], (to(cuts[q], i), feat))

    for off in around(n):
        for q in (0, 1):
            p4_copy(q, lax.rem(spot(cuts[q]) + off, n)).start()
    for q in (0, 1):
        wg_acc[spot(cuts[q]), q] = res[q]
    for q in (0, 1):
        left(p3_recv.at[q, 0 : n - 1], p3_ss.at[q])
    for q in (0, 1):
        left(wg_acc.at[0 : n - 1, q], p4_ss.at[q])
    for q in (0, 1):
        arrived(wg_acc.at[0 : n - 1, q], p4_rs.at[q])
        for i in range(n):
            for k in (0, 1):
                block = 2 * q + k
                wg_out[i * r : (i + 1) * r, block * TILE : (block + 1) * TILE] = wg_acc[i, q, k]


def solution(mesh):
    nx = mesh.shape["feat"] // 2
    n = round(mesh.shape["dp"] ** 0.5)

    def shards(source_feat, weight, tile_index, tile_count, tile_mask, cotangent):
        nblk, maxt, tile, _ = tile_mask.shape
        width = source_feat.shape[1]
        hid = weight.shape[1]
        rows = TILE // n
        half = n // 2
        bf16, f32 = jnp.bfloat16, jnp.float32
        dma = lambda *shape: pltpu.SemaphoreType.DMA(shape)
        vm = pltpu.VMEM
        hbm = pl.BlockSpec(memory_space=pltpu.HBM)
        vmem = pl.BlockSpec(memory_space=pltpu.VMEM)
        hidden, weight_grad = pl.pallas_call(
            functools.partial(kernel, nx, n, maxt, width),
            out_shape=(
                vm((tile, hid), bf16),
                vm((width, hid), f32),
            ),
            in_specs=[hbm] * 6,
            out_specs=(vmem, vmem),
            scratch_shapes=[
                pltpu.SMEM((maxt, nblk), jnp.int32),
                pltpu.SMEM((1, nblk), jnp.int32),
                vm((width, source_feat.shape[0]), bf16),
                vm((source_feat.shape[0] // tile, width + 16, tile), bf16),
                vm((nx, 2, maxt, tile, tile), jnp.int32),
                vm((half, rows, hid), bf16),
                vm((2, tile, hid), bf16),
                vm((min(3, nx), half, rows, hid), bf16),
                vm((2, nx, n, rows, TILE), bf16),
                vm((nx, width, 2 * tile), bf16),
                vm((nx, width, 2 * tile), bf16),
                vm((2 * tile, hid), bf16),
                vm((2 * tile, hid), bf16),
                vm((nx, TILE // 2, TILE), bf16),
                vm((nx, TILE // 2, TILE), bf16),
                vm((n, 2, nx // 2, rows, TILE), bf16),
                vm((n, 2, nx // 2, rows, TILE), bf16),
                vm((n, nx // 2, rows, TILE), bf16),
                vm((n, nx // 2, rows, TILE), bf16),
                vm((n, rows // 2, TILE), f32),
                vm((n, rows // 2, TILE), f32),
                vm((nx, 3, rows // 2, TILE), f32),
                vm((nx, 3, rows // 2, TILE), f32),
                vm((2, rows, TILE), bf16),
                vm((2, n, rows, TILE), bf16),
                vm((2, 2, rows // 2, TILE), f32),
                vm((n, 2, 2, rows // 2, TILE), f32),
                dma(2), dma(), dma(nx), dma(), dma(),
                dma(), dma(),
                dma(), dma(),
                dma(2), dma(2, 2),
                dma(2, 2), dma(2, 2),
                dma(), dma(),
                dma(), dma(),
                dma(), dma(),
                dma(), dma(),
                dma(), dma(),
                dma(), dma(),
                dma(), dma(),
                dma(2), dma(2),
                dma(2), dma(2),
            ],
            compiler_params=pltpu.CompilerParams(
                collective_id=0, has_side_effects=True, vmem_limit_bytes=40 * 1024 * 1024
            ),
        )(
            *(
                pltpu.with_memory_space_constraint(a, pltpu.HBM)
                for a in (
                    tile_index.T,
                    tile_count.reshape(1, nblk),
                    source_feat.T,
                    weight.reshape(half, rows, hid),
                    tile_mask,
                    cotangent,
                )
            )
        )
        return hidden, weight_grad

    in_specs = (
        P("dp", "feat"),
        P("feat", None),
        P("dp", None),
        P("dp"),
        P("dp", None, None, None),
        P(("dp", "feat"), None),
    )
    out_specs = (P(("dp", "feat"), None), P("feat", None))
    return jax.shard_map(shards, mesh=mesh, in_specs=in_specs, out_specs=out_specs, check_vma=False)
```

time: 60.1 us -> 58.6 us (0.975); the launches traced: 59.9 us -> 57.7 us
  Pallas kernels: 58 us -> 55.8 us
    pallas_call x1, Pallas kernels: 58 us -> 55.8 us  [shards(): pl.pallas_call(functools.partial(kernel, nx, n, maxt, width), out_shape=(...]
where the time goes in v4:
time: 58.6 us; the launch traced here: 57.7 us
  Pallas kernels  55.8 us (95%)
  local copies, waits for them, and re-layouts  1.31 us (2%)
  between operations  0.64 us (1%)
    pallas_call x1, Pallas kernels, shards(): pl.pallas_call(functools.partial(kernel, nx, n, maxt, width), out_shape=(...  55.8 us
    unnamed x2, local copies, waits for them, and re-layouts  1.31 us

profile of v4, /device:TPU:1, one launch (start us, length us, event | category | flops | bytes accessed | tf_op | source)
XLA Modules:
  0.0 57.7 jit_solution(17759321913551984924)
XLA Ops:
  0.6 55.8 %shard_map.77 = (bf16[128,512]{1,0:T(8,128)(2,1)S(1)}, f32[64,512]{1,0:T(8,128)S(1)}) custom-call(s32[8,16]{1,0:T(8,128)} %bitcast.6, s32[1,16]{1,0:T(1,128)} %bitcast.7, bf16[64,8192]{1,0:T(8,128)(2,1)} %bitcast.4, bf16[4,16,512]{2,1,0:T(8,128)(2,1)} %bitcast.5, s32[16,8,128,128]{3,2,1,0:T(8,128)} %mask.1, bf16[128,512]{1,0:T(8,128)(2,1)} %cot.1), custom_call_target="tpu_custom_call" | custom-call | tf_op jit(solution)/shard_map/pallas_call | solution.py:335
  56.4 0.7 %copy.10 = bf16[128,512]{1,0:T(8,128)(2,1)} copy(bf16[128,512]{1,0:T(8,128)(2,1)S(1)} %get-tuple-element.2) | data formatting | bytes 262144
  57.1 0.7 %copy.11 = f32[64,512]{1,0:T(8,128)} copy(f32[64,512]{1,0:T(8,128)S(1)} %get-tuple-element.3) | data formatting | bytes 262144

commit v5 on v4

--- a/solution.py
+++ b/solution.py
@@ -84,7 +84,7 @@
     get_ix = [pltpu.make_async_copy(a, b, ix_sem.at[i]) for i, (a, b) in enumerate(((tix_h, tix), (tcnt_h, tcnt)))]
     get_src = pltpu.make_async_copy(src, src_v, src_sem)
     get_cot = pltpu.make_async_copy(cot, cot_x.at[c], cot_sem)
-    for copy in (get_w, *get_ix, get_src):
+    for copy in (get_w, *get_ix, get_src, get_cot):
         copy.start()
     for k in range(2):
         mask_copy(jnp.int32(k)).start()
@@ -96,7 +96,6 @@
             greet((at(ab, lax.rem(place[ab] + off, n)), feat))
     for k in range(2, nx):
         mask_copy(jnp.int32(k)).start()
-    get_cot.start()
 
     def chip_at(steps):
         return lax.rem(x + nx + steps, nx)

time: 58.6 us -> 58.4 us (level)
  no operation moved by 1% of the time
where the time goes in v5:
time: 58.4 us; the launch traced here: 57.8 us
  Pallas kernels  55.9 us (96%)
  local copies, waits for them, and re-layouts  1.31 us (2%)
  between operations  0.64 us (1%)
    pallas_call x1, Pallas kernels, shards(): pl.pallas_call(functools.partial(kernel, nx, n, maxt, width), out_shape=(...  55.9 us
    unnamed x2, local copies, waits for them, and re-layouts  1.31 us

profile of v5, /device:TPU:1, one launch (start us, length us, event | category | flops | bytes accessed | tf_op | source)
XLA Modules:
  0.0 57.8 jit_solution(2989556594758918285)
XLA Ops:
  0.6 55.9 %shard_map.77 = (bf16[128,512]{1,0:T(8,128)(2,1)S(1)}, f32[64,512]{1,0:T(8,128)S(1)}) custom-call(s32[8,16]{1,0:T(8,128)} %bitcast.6, s32[1,16]{1,0:T(1,128)} %bitcast.7, bf16[64,8192]{1,0:T(8,128)(2,1)} %bitcast.4, bf16[4,16,512]{2,1,0:T(8,128)(2,1)} %bitcast.5, s32[16,8,128,128]{3,2,1,0:T(8,128)} %mask.1, bf16[128,512]{1,0:T(8,128)(2,1)} %cot.1), custom_call_target="tpu_custom_call" | custom-call | tf_op jit(solution)/shard_map/pallas_call | solution.py:334
  56.5 0.7 %copy.10 = bf16[128,512]{1,0:T(8,128)(2,1)} copy(bf16[128,512]{1,0:T(8,128)(2,1)S(1)} %get-tuple-element.2) | data formatting | bytes 262144
  57.2 0.7 %copy.11 = f32[64,512]{1,0:T(8,128)} copy(f32[64,512]{1,0:T(8,128)S(1)} %get-tuple-element.3) | data formatting | bytes 262144

commit v6 on v5

--- a/solution.py
+++ b/solution.py
@@ -260,11 +260,12 @@
     along(1 - c, lambda i: p2x_copy(i).start())
     lone_recv[spot(1 - c)] = lone_send[spot(1 - c)]
     arrived(lone_recv.at[0 : n - 1], lone_rs)
-    p2_send[:, 2] = jnp.sum(lone_recv[...].astype(f32), axis=0).reshape(nx, r, TILE)
+    lone = jnp.sum(lone_recv[...].astype(f32), axis=0).reshape(nx, r, TILE)
+    p2_send[:, 1] = jnp.concatenate([lone, lone], axis=1).astype(bf16)
     pair_recv[spot(c)] = pair_send[spot(c)]
     arrived(pair_recv.at[0 : n - 1], pair_rs)
-    for k in (0, 1):
-        p2_send[:, k] = jnp.sum(pair_recv[:, k].astype(f32), axis=0).reshape(nx, r, TILE)
+    pair = [jnp.sum(pair_recv[:, k].astype(f32), axis=0).reshape(nx, r, TILE) for k in (0, 1)]
+    p2_send[:, 0] = jnp.concatenate(pair, axis=1).astype(bf16)
     for slot in reversed(range(1, nx)):
         p2_copy(slot).start()
     left(p1x_send.at[1:nx], p1x_ss)
@@ -275,7 +276,8 @@
     group0 = jnp.sum(p2x_recv[...], axis=0)
     p2_recv[0] = p2_send[0]
     arrived(p2_recv.at[1:nx], p2_rs)
-    groups = jnp.sum(p2_recv[...], axis=0)
+    sums = jnp.sum(p2_recv[...].astype(f32), axis=0)
+    groups = sums[0, :r], sums[0, r:], sums[1, :r]
 
     cuts = (1 - c, c)
     pairs = ((group0, groups[2]), (groups[0], groups[1]))
@@ -361,8 +363,8 @@
                 vm((n, nx // 2, rows, TILE), bf16),
                 vm((n, rows // 2, TILE), f32),
                 vm((n, rows // 2, TILE), f32),
-                vm((nx, 3, rows // 2, TILE), f32),
-                vm((nx, 3, rows // 2, TILE), f32),
+                vm((nx, 2, rows, TILE), bf16),
+                vm((nx, 2, rows, TILE), bf16),
                 vm((2, rows, TILE), bf16),
                 vm((2, n, rows, TILE), bf16),
                 vm((2, 2, rows // 2, TILE), f32),

time: 58.4 us -> 57.9 us (level)
  Pallas kernels: 55.9 us -> 55.3 us
    pallas_call x1, Pallas kernels: 55.9 us -> 55.3 us  [shards(): pl.pallas_call(functools.partial(kernel, nx, n, maxt, width), out_shape=(...]
where the time goes in v6:
time: 57.9 us; the launch traced here: 57.2 us
  Pallas kernels  55.3 us (96%)
  local copies, waits for them, and re-layouts  1.31 us (2%)
  between operations  0.64 us (1%)
    pallas_call x1, Pallas kernels, shards(): pl.pallas_call(functools.partial(kernel, nx, n, maxt, width), out_shape=(...  55.3 us
    unnamed x2, local copies, waits for them, and re-layouts  1.31 us

profile of v6, /device:TPU:1, one launch (start us, length us, event | category | flops | bytes accessed | tf_op | source)
XLA Modules:
  0.0 57.2 jit_solution(15849350776772455747)
XLA Ops:
  0.6 55.3 %shard_map.77 = (bf16[128,512]{1,0:T(8,128)(2,1)S(1)}, f32[64,512]{1,0:T(8,128)S(1)}) custom-call(s32[8,16]{1,0:T(8,128)} %bitcast.6, s32[1,16]{1,0:T(1,128)} %bitcast.7, bf16[64,8192]{1,0:T(8,128)(2,1)} %bitcast.4, bf16[4,16,512]{2,1,0:T(8,128)(2,1)} %bitcast.5, s32[16,8,128,128]{3,2,1,0:T(8,128)} %mask.1, bf16[128,512]{1,0:T(8,128)(2,1)} %cot.1), custom_call_target="tpu_custom_call" | custom-call | tf_op jit(solution)/shard_map/pallas_call | solution.py:336
  55.9 0.7 %copy.10 = bf16[128,512]{1,0:T(8,128)(2,1)} copy(bf16[128,512]{1,0:T(8,128)(2,1)S(1)} %get-tuple-element.2) | data formatting | bytes 262144
  56.6 0.7 %copy.11 = f32[64,512]{1,0:T(8,128)} copy(f32[64,512]{1,0:T(8,128)S(1)} %get-tuple-element.3) | data formatting | bytes 262144
